TPU v7x, 128 devices: a whole 4x4x4 slice. The times are simulated.
128 devices in a mesh: head: 16 (over z, y), tok: 8 (over x, core).
Axes of the slice: x: 4, y: 4, z: 4, core: 2. Of those that a mesh axis runs over, the one named last changes fastest.
Arguments:
- queries: bfloat16 [2048, 8192], P('tok', 'head'), may hold values from -6 to 6
- cache: bfloat16 [4, 4096, 256], P(None, 'tok'), may hold values from -6 to 6
- new_kv: bfloat16 [4, 2048, 256], P(None, 'tok'), may hold values from -6 to 6
- q_gain: float32 [128], replicated, may hold values from 0.5 to 2.2
- k_gain: float32 [128], replicated, may hold values from 0.5 to 2.2
- out_weight: bfloat16 [8192, 4096], P('head'), may hold values from -0.5 to 0.5
- residual: bfloat16 [2048, 4096], P(('tok', 'head')), may hold values from -3 to 3
- norm_gain: float32 [4096], replicated, may hold values from 0.25 to 1.75
- expert_ids: int32 [2048, 8], P(('tok', 'head')), may hold values from 0 to 127, all different within a row; in each aligned block of 16 rows (0 to 15, 16 to 31, ...) at most 2 rows name the same one
- combine_weight: bfloat16 [2048, 8], P(('tok', 'head')), may hold values from 0.049804688 to 0.5
- prefix_len: int32 [1], replicated, may hold values from 2048 to 4096
- w_gate_up: bfloat16 [128, 4096, 1536], P(('head', 'tok')), may hold values from -0.09375 to 0.09375
- w_down: bfloat16 [128, 768, 4096], P(('head', 'tok')), may hold values from -0.21875 to 0.21875
Outputs:
- layer_out: bfloat16 [2048, 4096], P(('tok', 'head'))
Inputs may be any that keep to these rules, and one draw needn't show every extreme that they name: `expert_ids`: in each aligned block of 16 rows (the rows of one device) no expert is named by more than 2 rows, and some expert reaches 2.
All inputs are finite; a program needn't handle non-finite values.
Results may differ from a plain program's by a relative error of at most 0.022.
Values may be sent and summed in bfloat16 or wider, within the bound.
No kernel may reach another device: no remote copies, remote signals or barrier semaphores. Data moves between devices by JAX's collectives and lax.ppermute only.
A program may use at most 128 MiB of HBM per device.

v0:
```python
import jax
import jax.numpy as jnp
from jax import lax
from jax.sharding import PartitionSpec as P

HEADS = 64
KV_HEADS = 4
HD = 128


EPSILON = 1e-06


def rms_scale(values, gain):
    mean_square = jnp.mean(values * values, axis=-1, keepdims=True)
    return values * lax.rsqrt(mean_square + EPSILON) * gain


def expert_block(inputs, gate_up, down_proj):
    width = down_proj.shape[1]
    hidden_units = down_proj.shape[0]
    flat_rows = inputs.reshape(-1, width)
    both = jnp.dot(flat_rows, gate_up, preferred_element_type=jnp.float32)
    active = (jax.nn.silu(both[:, :hidden_units]) * both[:, hidden_units:]).astype(jnp.bfloat16)
    result = jnp.dot(active, down_proj, preferred_element_type=jnp.float32).astype(jnp.bfloat16)
    return result.reshape(inputs.shape)


def per_device(
    queries,
    cache,
    new_kv,
    q_gain,
    k_gain,
    out_weight,
    residual,
    norm_gain,
    expert_ids,
    combine_weight,
    prefix_len,
    w_gate_up,
    w_down,
):
    head_count = lax.axis_size("head")
    tok_count = lax.axis_size("tok")
    query_rows = queries.shape[0]
    local_heads = queries.shape[1] // HD
    cache_rows = cache.shape[1]
    segment = cache_rows + query_rows
    kv_index = lax.axis_index("head") * local_heads // (HEADS // KV_HEADS)
    query_normed = rms_scale(
        queries.reshape(query_rows, local_heads, HD).astype(jnp.float32), q_gain
    ).astype(jnp.bfloat16)
    own_block = jnp.concatenate(
        [
            lax.dynamic_index_in_dim(cache, kv_index, 0, keepdims=False),
            lax.dynamic_index_in_dim(new_kv, kv_index, 0, keepdims=False),
        ],
        axis=0,
    )
    key_part = rms_scale(own_block[:, :HD].astype(jnp.float32), k_gain).astype(jnp.bfloat16)
    key_block = jnp.concatenate([key_part, own_block[:, HD:]], axis=1)
    query_position = lax.axis_index("tok") * query_rows + jnp.arange(query_rows, dtype=jnp.int32)
    limit = prefix_len[0]
    piece = lax.all_gather(key_block, "tok", axis=0, tiled=True)
    position = jnp.arange(piece.shape[0], dtype=jnp.int32)
    shard = position // segment
    offset = position % segment
    in_cache = offset < cache_rows
    cache_position = shard * cache_rows + offset
    span_position = shard * query_rows + offset - cache_rows
    visible = jnp.where(
        in_cache[None, :],
        (cache_position < limit)[None, :],
        span_position[None, :] <= query_position[:, None],
    )
    scores = jnp.einsum(
        "qhd,kd->qhk", query_normed, piece[:, :HD], preferred_element_type=jnp.float32
    ) * HD ** (-0.5)
    weights = jnp.where(visible[:, None, :], jnp.exp(scores), 0.0)
    accum = jnp.einsum(
        "qhk,kd->qhd",
        weights.astype(jnp.bfloat16),
        piece[:, HD:],
        preferred_element_type=jnp.float32,
    )
    total = jnp.sum(weights, axis=2)
    accum, total = (accum, total)
    attn = (accum / total[:, :, None]).astype(jnp.bfloat16).reshape(query_rows, local_heads * HD)
    rows_out = query_rows // head_count
    full_proj = lax.psum(
        jnp.dot(attn, out_weight, preferred_element_type=jnp.float32).astype(jnp.bfloat16), "head"
    ).astype(jnp.float32)
    attn_proj = lax.dynamic_slice_in_dim(full_proj, lax.axis_index("head") * rows_out, rows_out, 0)
    hidden = residual.astype(jnp.float32) + attn_proj
    normed = rms_scale(hidden, norm_gain).astype(jnp.bfloat16)
    width = normed.shape[1]
    experts_all = head_count * tok_count
    topk = expert_ids.shape[1]
    capacity = max(2, 2 * rows_out * topk // experts_all)
    flat_ids = expert_ids.reshape(-1)
    onehot = (flat_ids[:, None] == jnp.arange(experts_all, dtype=jnp.int32)[None, :]).astype(
        jnp.int32
    )
    before = jnp.cumsum(onehot, axis=0) - onehot
    slot_index = jnp.sum(before * onehot, axis=1)
    target = (flat_ids * capacity + slot_index).reshape(rows_out, topk)
    matches = (
        target[:, :, None] == jnp.arange(experts_all * capacity, dtype=jnp.int32)[None, None, :]
    )
    placing = jnp.sum(matches.astype(jnp.int32), axis=1).astype(jnp.bfloat16)
    mixing = jnp.sum(
        jnp.where(matches, combine_weight.astype(jnp.float32)[:, :, None], 0.0), axis=1
    ).astype(jnp.bfloat16)
    outgoing = jnp.einsum("rs,rd->sd", placing, normed, preferred_element_type=jnp.float32).astype(
        jnp.bfloat16
    )
    outgoing = outgoing.reshape(experts_all, capacity, width)
    returned = lax.all_to_all(
        expert_block(
            lax.all_to_all(outgoing, ("head", "tok"), split_axis=0, concat_axis=0, tiled=True),
            w_gate_up[0],
            w_down[0],
        ),
        ("head", "tok"),
        split_axis=0,
        concat_axis=0,
        tiled=True,
    )
    back_rows = returned.reshape(experts_all * capacity, width)
    expert_sum = jnp.dot(mixing, back_rows, preferred_element_type=jnp.float32)
    return (hidden + expert_sum).astype(jnp.bfloat16)


def solution(mesh):
    placed = (
        P("tok", "head"),
        P(None, "tok", None),
        P(None, "tok", None),
        P(),
        P(),
        P("head", None),
        P(("tok", "head"), None),
        P(),
        P(("tok", "head"), None),
        P(("tok", "head"), None),
        P(),
        P(("head", "tok"), None, None),
        P(("head", "tok"), None, None),
    )
    return jax.shard_map(
        per_device, mesh=mesh, in_specs=placed, out_specs=P(("tok", "head"), None), check_vma=False
    )
```

profile of v0, /device:TPU:1, one launch (start us, length us, event | category | flops | bytes accessed | tf_op | source)
XLA Modules:
  0.0 266.1 jit_solution(3016336318144952375)
XLA Ops:
  6.6 1.2 copy-done
  7.8 0.9 dynamic-slice_bitcast_fusion.1
  8.9 0.8 fusion.25
  9.7 0.8 fusion.27
  11.5 0.3 multiply_reduce_fusion
  11.9 0.3 multiply_convert_fusion
  12.2 1.1 compare_select_fusion
  13.4 28.7 %all-gather.2.cloned.1.call-done = bf16[6144,256]{1,0:T(8,128)(2,1)} async-done(((bf16[768,256]{1,0:T(8,128)(2,1)}), bf16[6144,256]{1,0:T(8,128)(2,1)}) %all-gather.2.cloned.1.call-update) | async-done | bytes 3145744 | tf_op jit(solution)/shard_map/all_gather | solution.py:65
  42.0 13.0 %fusion = (f32[256,4]{0,1:T(4,128)S(1)}, f32[256,4,6144]{2,0,1:T(8,128)}) fusion(pred[256,6144]{1,0:T(8,128)(4,1)S(1)} %compare_select_fusion, bf16[6144,256]{1,0:T(8,128)(2,1)} %all-gather.2.cloned.1.call-done, bf16[256,4,128]{2,1,0:T(4,128)(2,1)S(1)} %multiply_convert_fusion), kind=kOutput, calls=%fused_computation.1 | convolution fusion | flops 1629486080 | bytes 28577792 | tf_op jit(solution)/shard_map/qhd,kd->qhk/dot_general | solution.py:77
  55.0 11.2 %fusion.17 = bf16[256,4,128]{0,2,1:T(8,128)(2,1)S(1)} fusion(bf16[6144,256]{1,0:T(8,128)(2,1)} %all-gather.2.cloned.1.call-done, f32[256,4,6144]{2,0,1:T(8,128)} %get-tuple-element.6, pred[256,6144]{1,0:T(8,128)(4,1)S(1)} %compare_select_fusion, f32[256,4]{0,1:T(4,128)S(1)} %get-tuple-element.5), kind=kOutput, calls=%fused_computation.19 | convolution fusion | flops 1629749248 | bytes 28577792 | tf_op jit(solution)/shard_map/qhk,kd->qhd/dot_general | solution.py:81
  66.3 2.6 convolution_convert_fusion.1
  69.8 88.4 %all-reduce.2.cloned.1.call-done = bf16[256,4096]{1,0:T(8,128)(2,1)} async-done(((bf16[256,4096]{1,0:T(8,128)(2,1)}), bf16[256,4096]{1,0:T(8,128)(2,1)}) %all-reduce.2.cloned.1.call-update) | async-done | bytes 2097168 | tf_op jit(solution)/shard_map/psum | solution.py:91
  158.2 1.1 multiply_reduce_fusion.1
  159.2 1.7 convolution_convert_fusion
  160.9 2.7 %reshape.136 = bf16[128,2,4096]{2,1,0:T(2,128)(2,1)} reshape(bf16[256,4096]{1,0:T(8,128)(2,1)S(1)} %convolution_convert_fusion) | data formatting | bytes 4194304 | tf_op jit(solution)/shard_map/reshape | solution.py:118
  163.6 39.1 %all_to_all.10 = bf16[128,2,4096]{2,1,0:T(2,128)(2,1)S(1)} all-to-all(bf16[128,2,4096]{2,1,0:T(2,128)(2,1)} %reshape.136), channel_id=1, replica_groups=mesh['head'=16,'tok'=8] {'head','tok'}, dimensions={0} | all-to-all | bytes 4194304 | tf_op jit(solution)/shard_map/all_to_all | solution.py:121
  202.7 2.2 reshape.137
  204.9 7.0 %fusion.2 = f32[256,1536]{1,0:T(8,128)S(1)} fusion(bf16[256,4096]{1,0:T(8,128)(2,1)} %reshape.137, bf16[1,4096,1536]{2,1,0:T(8,128)(2,1)} %param.24), kind=kOutput, calls=%fused_computation.3 | convolution fusion | flops 3221225472 | bytes 16252928 | tf_op jit(solution)/shard_map/dot_general | solution.py:23
  212.0 4.6 %fusion.9 = bf16[256,4096]{1,0:T(8,128)(2,1)S(1)} fusion(bf16[1,768,4096]{2,1,0:T(8,128)(2,1)} %param.25, f32[256,1536]{1,0:T(8,128)S(1)} %fusion.2), kind=kOutput, calls=%fused_computation.12 | convolution fusion | flops 1612840960 | bytes 9961472 | tf_op jit(solution)/shard_map/dot_general | solution.py:25
  216.6 2.7 %reshape.138 = bf16[128,2,4096]{2,1,0:T(2,128)(2,1)} reshape(bf16[256,4096]{1,0:T(8,128)(2,1)S(1)} %fusion.9) | data formatting | bytes 4194304 | tf_op jit(solution)/shard_map/reshape | solution.py:26
  219.3 4.5 %all-to-all-start.1 = ((bf16[128,2,4096]{2,1,0:T(2,128)(2,1)}), bf16[128,2,4096]{2,1,0:T(2,128)(2,1)S(1)}, u32[]{:S(2)}, u32[]{:S(2)}) async-start(bf16[128,2,4096]{2,1,0:T(2,128)(2,1)} %reshape.138), calls=%async_computation.1 | async-start | bytes 4194304 | tf_op jit(solution)/shard_map/all_to_all | solution.py:119
  224.0 30.4 %all-to-all-done.1 = bf16[128,2,4096]{2,1,0:T(2,128)(2,1)S(1)} async-done(((bf16[128,2,4096]{2,1,0:T(2,128)(2,1)}), bf16[128,2,4096]{2,1,0:T(2,128)(2,1)S(1)}, u32[]{:S(2)}, u32[]{:S(2)}) %all-to-all-start.1) | async-done | bytes 2097184 | tf_op jit(solution)/shard_map/all_to_all | solution.py:119
  254.4 2.2 reshape.139
  256.7 2.6 fusion.12
  (40 shorter events, 1.6 us)
Async XLA Ops:
  6.5 1.2 copy-start
  6.5 4.7 %copy-start.4 = (bf16[256,512]{1,0:T(8,128)(2,1)S(1)}, bf16[256,512]{1,0:T(8,128)(2,1)}, u32[]{:S(2)}) copy-start(bf16[256,512]{1,0:T(8,128)(2,1)} %param.13) | copy-start | bytes 786436
  6.5 5.3 %copy-start.8 = (f32[128]{0:T(128)S(1)}, f32[128]{0:T(128)}, u32[]{:S(2)}) copy-start(f32[128]{0:T(128)} %param.16) | copy-start | bytes 1540
  6.5 35.5 %all-gather.2.cloned.1.call-start = ((), (), s32[]{:S(2)}) async-start(), calls=%async_computation.2 | async-start | bytes 3538944 | tf_op jit(solution)/shard_map/all_gather | solution.py:65
  10.5 147.6 %all-reduce.2.cloned.1.call-start = ((), (), s32[]{:S(2)}) async-start(), calls=%async_computation.3 | async-start | bytes 4194304 | tf_op jit(solution)/shard_map/psum | solution.py:91
  55.0 11.2 %copy-start.2 = (bf16[512,4096]{1,0:T(8,128)(2,1)S(1)}, bf16[512,4096]{1,0:T(8,128)(2,1)}, u32[]{:S(2)}) copy-start(bf16[512,4096]{1,0:T(8,128)(2,1)} %param.18) | copy-start | bytes 12582916
  66.3 2.7 %copy-start.6 = (s32[16,8]{0,1:T(8,128)S(1)}, s32[16,8]{0,1:T(8,128)}, u32[]{:S(2)}) copy-start(s32[16,8]{0,1:T(8,128)} %param.21) | copy-start | bytes 1540
  66.3 91.9 %copy-start.3 = (bf16[16,4096]{1,0:T(8,128)(2,1)S(1)}, bf16[16,4096]{1,0:T(8,128)(2,1)}, u32[]{:S(2)}) copy-start(bf16[16,4096]{1,0:T(8,128)(2,1)} %param.19) | copy-start | bytes 393220
  66.3 92.9 %copy-start.5 = (f32[4096]{0:T(1024)S(1)}, f32[4096]{0:T(1024)}, u32[]{:S(2)}) copy-start(f32[4096]{0:T(1024)} %param.20) | copy-start | bytes 49156
  219.3 4.5 %copy-start.7 = (bf16[16,8]{0,1:T(8,128)(2,1)S(1)}, bf16[16,8]{0,1:T(8,128)(2,1)}, u32[]{:S(2)}) copy-start(bf16[16,8]{0,1:T(8,128)(2,1)} %param.22) | copy-start | bytes 772
  219.3 35.2 %all-to-all-start.1 = ((bf16[128,2,4096]{2,1,0:T(2,128)(2,1)}), bf16[128,2,4096]{2,1,0:T(2,128)(2,1)S(1)}, u32[]{:S(2)}, u32[]{:S(2)}) async-start(bf16[128,2,4096]{2,1,0:T(2,128)(2,1)} %reshape.138), calls=%async_computation.1 | async-start | bytes 4194304 | tf_op jit(solution)/shard_map/all_to_all | solution.py:119
  223.9 35.4 %copy-start.1 = (bf16[4,512,256]{2,1,0:T(8,128)(2,1)S(1)}, bf16[4,512,256]{2,1,0:T(8,128)(2,1)}, u32[]{:S(2)}) copy-start(bf16[4,512,256]{2,1,0:T(8,128)(2,1)} %param.14) | copy-start | bytes 3145732
Sparse Core Ops, SparseCore 0:
  10.7 31.3 all-gather.1
  69.0 89.0 all-reduce.1
where the time goes:
time: 267 us; the launch traced here: 266 us
  waiting for transfers between devices  148 us (55%)
  matrix products  42.8 us (16%)
  blocking collectives  39.1 us (15%)
  between operations  14.3 us (5%)
  local copies, waits for them, and re-layouts  12.4 us (5%)
  other arithmetic  5.43 us (2%)
  starting transfers between devices  4.54 us (2%)
    psum x1, waiting for transfers between devices, per_device(): lax.psum(jnp.dot(attn, out_weight, preferred_element_type=jnp.float32).as...  88.4 us
    all_to_all x1, blocking collectives, per_device(): lax.all_to_all(outgoing, ('head', 'tok'), split_axis=0, concat_axis=0, ti...  39.1 us
    all_to_all x1, waiting for transfers between devices, per_device(): lax.all_to_all(expert_block(lax.all_to_all(outgoing, ('head', 'tok'), spl...  30.4 us
    all_gather x1, waiting for transfers between devices, per_device(): piece = lax.all_gather(key_block, 'tok', axis=0, tiled=True)  28.7 us
    dot_general x1, matrix products, per_device(): jnp.einsum('qhd,kd->qhk', query_normed, piece[:, :HD], preferred_element_...  13 us
    dot_general x1, matrix products, per_device(): jnp.einsum('qhk,kd->qhd', weights.astype(jnp.bfloat16), piece[:, HD:], pr...  11.2 us
    dot_general x1, matrix products, expert_block(): both = jnp.dot(flat_rows, gate_up, preferred_element_type=jnp.float32)  7.02 us
  transfers between devices with their start and end apart: 3, of which 3 were waited for; matrix products, arithmetic and copies ran while one was open for 1% of the time, Pallas kernels for 0%

commit v1 on v0

v1 whole, which is shorter than its diff:
```python
import functools
import math

import jax
import jax.numpy as jnp
from jax import lax
from jax.experimental import pallas as pl
from jax.experimental.pallas import tpu as pltpu
from jax.sharding import Mesh
from jax.sharding import PartitionSpec as P

HEADS = 64
KV_HEADS = 4
HD = 128
WIDTH = 4096
HALF = WIDTH // 2
ROWS = 16
QROWS = 256
QHEADS = 4
CACHE_ROWS = 512
SHARD = CACHE_ROWS + QROWS
SHARDS = 8
EXPERTS = 128
SLOTS = 2
CHUNKS = 8
PIECE = WIDTH // CHUNKS
LINES = CHUNKS * SLOTS
FFE = 768
GROUP = 16
GROUP_LINES = GROUP * LINES
EPSILON = 1e-06
SCALE = math.log2(math.e) / math.sqrt(HD)
MB = 1 << 20

F32 = jnp.float32
BF16 = jnp.bfloat16

VMEM = functools.partial(pl.BlockSpec, memory_space=pltpu.VMEM)
SMEM = functools.partial(pl.BlockSpec, memory_space=pltpu.SMEM)
ANY = functools.partial(pl.BlockSpec, memory_space=pl.ANY)


def params(limit):
    return pltpu.CompilerParams(vmem_limit_bytes=limit * MB)


def rms_scale(values, gain):
    mean_square = jnp.mean(values * values, axis=-1, keepdims=True)
    return values * lax.rsqrt(mean_square + EPSILON) * gain


def shift(step):
    return [(i, (i + step) % 4) for i in range(4)]


def prep_kernel(kv_ref, cache_ref, new_ref, gain_ref, out_ref):
    for ref, start, rows in ((cache_ref, 0, CACHE_ROWS), (new_ref, CACHE_ROWS, QROWS)):
        keys = rms_scale(ref[:, :HD].astype(F32), gain_ref[...]).astype(BF16)
        out_ref[pl.ds(start, rows), :HD] = keys
        out_ref[pl.ds(start, rows), HD:] = ref[:, HD:]


def prep(kv_index, cache, new_kv, k_gain):
    return pl.pallas_call(
        prep_kernel,
        grid_spec=pltpu.PrefetchScalarGridSpec(
            num_scalar_prefetch=1,
            grid=(1,),
            in_specs=[
                pl.BlockSpec((None, CACHE_ROWS, 2 * HD), lambda i, kv: (kv[0], 0, 0)),
                pl.BlockSpec((None, QROWS, 2 * HD), lambda i, kv: (kv[0], 0, 0)),
                pl.BlockSpec((1, HD), lambda i, kv: (0, 0)),
            ],
            out_specs=pl.BlockSpec((SHARD, 2 * HD), lambda i, kv: (0, 0)),
        ),
        out_shape=jax.ShapeDtypeStruct((SHARD, 2 * HD), BF16),
        compiler_params=params(8),
    )(kv_index, cache, new_kv, k_gain)


def attention_kernel(
    place_ref, q_ref, gain_ref, *rest
):
    shards, rest = rest[:SHARDS], rest[SHARDS:]
    weight_ref, rest = rest[0], rest[1:]
    out_a, out_b, rest = rest[:4], rest[4:8], rest[8:]
    qn, kv, weight, acc, total, attn, result, kv_sem, weight_sem = rest
    limit, z, y, x, c = (place_ref[i] for i in range(5))
    tok = x * 2 + c
    copies = []
    for i in range(SHARDS):
        core = c if i < 4 else 1 - c
        owner = ((x + 4 - i % 4) % 4) * 2 + core
        copies.append(pltpu.make_async_copy(shards[i], kv.at[owner], kv_sem.at[i]))
    weight_copy = pltpu.make_async_copy(weight_ref, weight, weight_sem)
    for copy in copies:
        copy.start()
    weight_copy.start()
    for h in range(QHEADS):
        head = q_ref[:, h * HD : (h + 1) * HD].astype(F32)
        qn[pl.ds(h * QROWS, QROWS), :] = rms_scale(head, gain_ref[...]).astype(BF16)
    acc[...] = jnp.zeros_like(acc)
    total[...] = jnp.zeros_like(total)
    for copy in copies:
        copy.wait()

    def block(owner, start, rows, mask):
        keys = kv[owner, pl.ds(start, rows), :HD]
        values = kv[owner, pl.ds(start, rows), HD:]
        for h in range(QHEADS):
            at = pl.ds(h * QROWS, QROWS)
            scores = lax.dot_general(
                qn[at, :], keys, (((1,), (1,)), ((), ())), preferred_element_type=F32
            )
            weights = jnp.exp2(scores * SCALE)
            if mask is not None:
                weights = jnp.where(mask, weights, 0.0)
            part = weights[:, :HD]
            for i in range(1, rows // HD):
                part = part + weights[:, i * HD : (i + 1) * HD]
            total[at, :] += part
            acc[at, :] += jnp.dot(weights.astype(BF16), values, preferred_element_type=F32)

    full = limit // CACHE_ROWS

    @pl.loop(0, full)
    def _(owner):
        block(owner, 0, CACHE_ROWS, None)

    @pl.when(limit % CACHE_ROWS != 0)
    def _():
        position = lax.broadcasted_iota(jnp.int32, (QROWS, CACHE_ROWS), 1) + full * CACHE_ROWS
        block(full, 0, CACHE_ROWS, position < limit)

    @pl.loop(0, tok)
    def _(owner):
        block(owner, CACHE_ROWS, QROWS, None)

    key = lax.broadcasted_iota(jnp.int32, (QROWS, QROWS), 1)
    query = lax.broadcasted_iota(jnp.int32, (QROWS, QROWS), 0)
    block(tok, CACHE_ROWS, QROWS, key <= query)

    for h in range(QHEADS):
        at = pl.ds(h * QROWS, QROWS)
        whole = jnp.sum(total[at, :], axis=1, keepdims=True)
        attn[:, h * HD : (h + 1) * HD] = (acc[at, :] / whole).astype(BF16)
    weight_copy.wait()
    for n in range(8):
        columns = slice(n * 512, (n + 1) * 512)
        product = jnp.dot(attn[...], weight[:, columns], preferred_element_type=F32)
        result[:, :, columns] = product.astype(BF16).reshape(16, ROWS, 512)
    for k in range(4):
        for i in range(4):
            out_a[k][i] = result[i * 4 + (y + k) % 4, :, :HALF]
            out_b[k][i] = result[((z + k) % 4) * 4 + i, :, HALF:]


def attention(place, queries, q_gain, shards, weight):
    part = jax.ShapeDtypeStruct((4, ROWS, HALF), BF16)
    return pl.pallas_call(
        attention_kernel,
        in_specs=[SMEM(), VMEM(), VMEM()] + [ANY()] * (SHARDS + 1),
        out_specs=[VMEM()] * 8,
        out_shape=[part] * 8,
        scratch_shapes=[
            pltpu.VMEM((QHEADS * QROWS, HD), BF16),
            pltpu.VMEM((SHARDS, SHARD, 2 * HD), BF16),
            pltpu.VMEM((QHEADS * HD, WIDTH), BF16),
            pltpu.VMEM((QHEADS * QROWS, HD), F32),
            pltpu.VMEM((QHEADS * QROWS, HD), F32),
            pltpu.VMEM((QROWS, QHEADS * HD), BF16),
            pltpu.VMEM((16, ROWS, WIDTH), BF16),
            pltpu.SemaphoreType.DMA((SHARDS,)),
            pltpu.SemaphoreType.DMA,
        ],
        compiler_params=params(28),
    )(place, queries, q_gain, *shards, weight)


def sum_kernel(place_ref, *refs):
    parts_a, parts_b, refs = refs[:4], refs[4:8], refs[8:]
    out_a, out_b, (held_a, held_b) = refs[:4], refs[4:8], refs[8:]
    z, y = place_ref[1], place_ref[2]
    for parts, held in ((parts_a, held_a), (parts_b, held_b)):
        for i in range(4):
            value = parts[0][i].astype(F32)
            for other in parts[1:]:
                value = value + other[i].astype(F32)
            held[i] = value.astype(BF16)
    for k in range(4):
        out_a[k][...] = held_a[(z + k) % 4]
        out_b[k][...] = held_b[(y + k) % 4]


def first_sum(place, parts):
    row = jax.ShapeDtypeStruct((ROWS, HALF), BF16)
    return pl.pallas_call(
        sum_kernel,
        in_specs=[SMEM()] + [VMEM()] * 8,
        out_specs=[VMEM()] * 8,
        out_shape=[row] * 8,
        scratch_shapes=[pltpu.VMEM((4, ROWS, HALF), BF16)] * 2,
        compiler_params=params(12),
    )(place, *parts)


def route_kernel(columns_ref, rows_ref, mix_ref, placing_ref, mixing_ref):
    line = lax.broadcasted_iota(jnp.int32, (EXPERTS * LINES, EXPERTS), 0)
    lane = lax.broadcasted_iota(jnp.int32, (EXPERTS * LINES, EXPERTS), 1)
    slot = (line // LINES) * SLOTS + line % SLOTS
    hit = slot == columns_ref[0:1, :]
    for k in range(1, 8):
        hit = hit | (slot == columns_ref[k : k + 1, :])
    hit = hit & ((line // SLOTS) % CHUNKS == lane // ROWS)
    placing_ref[...] = jnp.where(hit, 1.0, 0.0).astype(BF16)
    line = lax.broadcasted_iota(jnp.int32, (EXPERTS, EXPERTS * LINES), 1)
    row = lax.broadcasted_iota(jnp.int32, (EXPERTS, EXPERTS * LINES), 0)
    slot = (line // LINES) * SLOTS + line % SLOTS
    value = jnp.zeros(slot.shape, F32)
    for k in range(8):
        value = jnp.where(slot == rows_ref[:, k : k + 1], mix_ref[:, k : k + 1], value)
    same = (line // SLOTS) % CHUNKS == row // ROWS
    mixing_ref[...] = jnp.where(same, value, 0.0).astype(BF16)


def route(expert_ids, combine_weight):
    flat = expert_ids.reshape(-1)
    index = jnp.arange(flat.shape[0], dtype=jnp.int32)
    earlier = (flat[:, None] == flat[None, :]) & (index[None, :] < index[:, None])
    slot = jnp.sum(earlier.astype(jnp.int32), axis=1)
    target = (flat * SLOTS + slot).reshape(expert_ids.shape)
    return pl.pallas_call(
        route_kernel,
        in_specs=[VMEM()] * 3,
        out_specs=[VMEM()] * 2,
        out_shape=[
            jax.ShapeDtypeStruct((EXPERTS * LINES, EXPERTS), BF16),
            jax.ShapeDtypeStruct((EXPERTS, EXPERTS * LINES), BF16),
        ],
        compiler_params=params(12),
    )(
        jnp.tile(target.T, (1, CHUNKS)),
        jnp.tile(target, (CHUNKS, 1)),
        jnp.tile(combine_weight.astype(F32), (CHUNKS, 1)),
    )


def dispatch_kernel(*refs):
    parts_a, parts_b, refs = refs[:4], refs[4:8], refs[8:]
    residual_ref, gain_ref, placing_ref, hidden_ref, out_ref, pieces = refs
    for parts, start in ((parts_a, 0), (parts_b, HALF)):
        value = parts[0][...].astype(F32)
        for other in parts[1:]:
            value = value + other[...].astype(F32)
        columns = slice(start, start + HALF)
        hidden_ref[:, columns] = residual_ref[:, columns].astype(F32) + value
    normed = rms_scale(hidden_ref[...], gain_ref[...]).astype(BF16)
    for k in range(CHUNKS):
        pieces[pl.ds(k * ROWS, ROWS), :] = normed[:, k * PIECE : (k + 1) * PIECE]
    for g in range(8):
        lines = jnp.dot(
            placing_ref[pl.ds(g * GROUP_LINES, GROUP_LINES), :],
            pieces[...],
            preferred_element_type=F32,
        )
        out_ref[pl.ds(g * GROUP, GROUP)] = lines.astype(BF16).reshape(GROUP, LINES, PIECE)


def dispatch(parts, residual, norm_gain, placing):
    return pl.pallas_call(
        dispatch_kernel,
        in_specs=[VMEM()] * 11,
        out_specs=[VMEM()] * 2,
        out_shape=[
            jax.ShapeDtypeStruct((ROWS, WIDTH), F32),
            jax.ShapeDtypeStruct((EXPERTS, LINES, PIECE), BF16),
        ],
        scratch_shapes=[pltpu.VMEM((EXPERTS, PIECE), BF16)],
        compiler_params=params(12),
    )(*parts, residual, norm_gain, placing)


def expert_kernel(lines_ref, up_ref, down_ref, out_ref, rows, both, active, back):
    size = (GROUP_LINES, GROUP_LINES)
    first = lax.broadcasted_iota(jnp.int32, size, 0)
    second = lax.broadcasted_iota(jnp.int32, size, 1)
    span = GROUP * SLOTS

    def held(by_chunk, by_source):
        source = (by_chunk % span) // SLOTS
        line = source * LINES + (by_chunk // span) * SLOTS + by_chunk % SLOTS
        return jnp.where(line == by_source, 1.0, 0.0).astype(BF16)

    gather, scatter = held(first, second), held(second, first)
    for g in range(8):
        group = lines_ref[pl.ds(g * GROUP, GROUP)].reshape(GROUP_LINES, PIECE)
        sorted_lines = jnp.dot(gather, group, preferred_element_type=F32).astype(BF16)
        for k in range(CHUNKS):
            rows[pl.ds(g * span, span), k * PIECE : (k + 1) * PIECE] = sorted_lines[
                k * span : (k + 1) * span, :
            ]
    for n in range(2 * FFE // 256):
        columns = slice(n * 256, (n + 1) * 256)
        both[:, columns] = jnp.dot(rows[...], up_ref[:, columns], preferred_element_type=F32)
    gate = both[:, :FFE]
    active[...] = (gate * jax.nn.sigmoid(gate) * both[:, FFE:]).astype(BF16)
    for k in range(CHUNKS):
        columns = slice(k * PIECE, (k + 1) * PIECE)
        down = jnp.dot(active[...], down_ref[:, columns], preferred_element_type=F32)
        down = down.astype(BF16)
        for g in range(8):
            back[g, pl.ds(k * span, span), :] = down[g * span : (g + 1) * span, :]
    for g in range(8):
        lines = jnp.dot(scatter, back[g], preferred_element_type=F32).astype(BF16)
        out_ref[pl.ds(g * GROUP, GROUP)] = lines.reshape(GROUP, LINES, PIECE)


def experts(lines, gate_up, down):
    return pl.pallas_call(
        expert_kernel,
        in_specs=[VMEM()] * 3,
        out_specs=VMEM(),
        out_shape=jax.ShapeDtypeStruct((EXPERTS, LINES, PIECE), BF16),
        scratch_shapes=[
            pltpu.VMEM((EXPERTS * SLOTS, WIDTH), BF16),
            pltpu.VMEM((EXPERTS * SLOTS, 2 * FFE), F32),
            pltpu.VMEM((EXPERTS * SLOTS, FFE), BF16),
            pltpu.VMEM((8, GROUP_LINES, PIECE), BF16),
        ],
        compiler_params=params(40),
    )(lines, gate_up, down)


def combine_kernel(lines_ref, mixing_ref, hidden_ref, out_ref):
    lines = lines_ref[...].reshape(EXPERTS * LINES, PIECE)
    mixed = jnp.dot(mixing_ref[...], lines, preferred_element_type=F32)
    for k in range(CHUNKS):
        columns = slice(k * PIECE, (k + 1) * PIECE)
        value = hidden_ref[:, columns] + mixed[k * ROWS : (k + 1) * ROWS, :]
        out_ref[:, columns] = value.astype(BF16)


def combine(lines, mixing, hidden):
    return pl.pallas_call(
        combine_kernel,
        in_specs=[VMEM()] * 3,
        out_specs=VMEM(),
        out_shape=jax.ShapeDtypeStruct((ROWS, WIDTH), BF16),
        compiler_params=params(12),
    )(lines, mixing, hidden)


def per_device(
    queries,
    cache,
    new_kv,
    q_gain,
    k_gain,
    out_weight,
    residual,
    norm_gain,
    expert_ids,
    combine_weight,
    prefix_len,
    w_gate_up,
    w_down,
):
    z, y, x, c = (lax.axis_index(name).astype(jnp.int32) for name in ("z", "y", "x", "c"))
    place = jnp.stack([prefix_len[0], z, y, x, c])
    own = prep(z.reshape(1), cache, new_kv, k_gain.reshape(1, HD))
    swap = functools.partial(lax.ppermute, axis_name="c", perm=[(0, 1), (1, 0)])
    near = [own] + [lax.ppermute(own, "x", shift(k)) for k in (1, 2, 3)]
    shards = near + [swap(shard) for shard in near]
    placing, mixing = route(expert_ids, combine_weight)
    queries, placing, mixing = lax.optimization_barrier((queries, placing, mixing))
    parts = attention(place, queries, q_gain.reshape(1, HD), shards, out_weight)
    part_a = [parts[0]] + [lax.ppermute(parts[k], "y", shift(k)) for k in (1, 2, 3)]
    part_b = [parts[4]] + [lax.ppermute(parts[4 + k], "z", shift(k)) for k in (1, 2, 3)]
    parts = first_sum(place, part_a + part_b)
    part_a = [parts[0]] + [lax.ppermute(parts[k], "z", shift(k)) for k in (1, 2, 3)]
    part_b = [parts[4]] + [lax.ppermute(parts[4 + k], "y", shift(k)) for k in (1, 2, 3)]
    hidden, lines = dispatch(
        part_a + part_b, residual, norm_gain.reshape(1, WIDTH), placing
    )
    everyone = ("z", "y", "x", "c")
    lines = lax.all_to_all(lines, everyone, split_axis=0, concat_axis=0, tiled=True)
    lines = experts(lines, w_gate_up[0], w_down[0])
    lines = lax.all_to_all(lines, everyone, split_axis=0, concat_axis=0, tiled=True)
    return combine(lines, mixing, hidden)


def solution(mesh):
    fine = Mesh(mesh.devices.reshape(4, 4, 4, 2), ("z", "y", "x", "c"))
    head, tok = ("z", "y"), ("x", "c")
    placed = (
        P(tok, head),
        P(None, tok, None),
        P(None, tok, None),
        P(),
        P(),
        P(head, None),
        P(tok + head, None),
        P(),
        P(tok + head, None),
        P(tok + head, None),
        P(),
        P(head + tok, None, None),
        P(head + tok, None, None),
    )
    return jax.shard_map(
        per_device, mesh=fine, in_specs=placed, out_specs=P(tok + head, None), check_vma=False
    )
```

time: 267 us -> 172 us (0.64)
  waiting for transfers between devices: 148 us -> 20.8 us
  matrix products: 42.8 us -> 0 us
  blocking collectives: 39.1 us -> 75.9 us
  starting transfers between devices: 4.54 us -> 36.2 us
  Pallas kernels: 0 us -> 29.5 us
  between operations: 14.3 us -> 0.81 us
  other arithmetic: 5.43 us -> 0.19 us
  local copies, waits for them, and re-layouts: 12.4 us -> 8.03 us
    psum x1 -> x0, waiting for transfers between devices: 88.4 us -> none  [per_device(): lax.psum(jnp.dot(attn, out_weight, preferred_element_type=jnp.float32).as...]
    dot_general x7 -> x0, matrix products: 42.8 us -> none  [the longest x1 13 us: per_device(): jnp.einsum('qhd,kd->qhk', query_normed, piece[:, :HD], preferred_element_...]
    all_to_all x1 -> x2, blocking collectives: 39.1 us -> 75.9 us  [per_device(): lax.all_to_all(lines, everyone, split_axis=0, concat_axis=0, tiled=True)]
    ppermute x0 -> x19, starting transfers between devices: none -> 36.2 us  [the longest x4 10.8 us: per_device(): shards = near + [swap(shard) for shard in near]]
    all_to_all x1 -> x0, waiting for transfers between devices: 30.4 us -> none  [per_device(): lax.all_to_all(expert_block(lax.all_to_all(outgoing, ('head', 'tok'), spl...]
    pallas_call x0 -> x7, Pallas kernels: none -> 29.5 us  [the longest x1 13.1 us: attention(): pl.pallas_call(attention_kernel, in_specs=[SMEM(), VMEM(), VMEM()] + [ANY...]
    all_gather x1 -> x0, waiting for transfers between devices: 28.7 us -> none  [per_device(): piece = lax.all_gather(key_block, 'tok', axis=0, tiled=True)]
    ppermute x0 -> x19, waiting for transfers between devices: none -> 20.8 us  [the longest x3 9.65 us: per_device(): near = [own] + [lax.ppermute(own, 'x', shift(k)) for k in (1, 2, 3)]]
  transfers between devices with their start and end apart: 3 -> 19, of which waited for: 3 -> 7; matrix products, arithmetic and copies ran while one was open for 1% -> 1% of each run, Pallas kernels for 0% -> 2%
where the time goes in v1:
time: 172 us; the launch traced here: 171 us
  blocking collectives  75.9 us (44%)
  starting transfers between devices  36.2 us (21%)
  Pallas kernels  29.5 us (17%)
  waiting for transfers between devices  20.8 us (12%)
  local copies, waits for them, and re-layouts  8.03 us (5%)
    all_to_all x2, blocking collectives, per_device(): lax.all_to_all(lines, everyone, split_axis=0, concat_axis=0, tiled=True)  75.9 us
    pallas_call x1, Pallas kernels, attention(): pl.pallas_call(attention_kernel, in_specs=[SMEM(), VMEM(), VMEM()] + [ANY...  13.1 us
    pallas_call x1, Pallas kernels, experts(): pl.pallas_call(expert_kernel, in_specs=[VMEM()] * 3, out_specs=VMEM(), ou...  10.8 us
    ppermute x4, starting transfers between devices, per_device(): shards = near + [swap(shard) for shard in near]  10.8 us
    ppermute x3, waiting for transfers between devices, per_device(): near = [own] + [lax.ppermute(own, 'x', shift(k)) for k in (1, 2, 3)]  9.65 us
    ppermute x3, starting transfers between devices, per_device(): lax.ppermute(parts[4 + k], 'z', shift(k))  7.85 us
    unnamed x21, local copies, waits for them, and re-layouts  6.85 us
    ppermute x3, waiting for transfers between devices, per_device(): lax.ppermute(parts[4 + k], 'z', shift(k))  5.82 us
  transfers between devices with their start and end apart: 19, of which 7 were waited for; matrix products, arithmetic and copies ran while one was open for 1% of the time, Pallas kernels for 2%

profile of v1, /device:TPU:1, one launch (start us, length us, event | category | flops | bytes accessed | tf_op | source)
XLA Modules:
  0.0 171.5 jit_solution(2083622831549464992)
XLA Ops:
  0.0 1.2 copy-done.1
  3.1 3.4 %collective-permute-start.2 = (bf16[768,256]{1,0:T(8,128)(2,1)S(1)}, bf16[768,256]{1,0:T(8,128)(2,1)}, u32[]{:S(2)}, u32[]{:S(2)}) collective-permute-start(bf16[768,256]{1,0:T(8,128)(2,1)S(1)} %shard_map.128.rest_0_), channel_id=1, source_target_pairs={{0,6},{2,0},{4,2},{6,4},{1,7},{3,1},{5,3},{7,5},{8,14},{10,8},{12,... | collective-permute-start | bytes 1179656 | tf_op jit(solution)/shard_map/ppermute | solution.py:372
  7.6 1.5 collective-permute-start.3
  9.2 6.3 %collective-permute-done.2.rest_3_ = bf16[768,256]{1,0:T(8,128)(2,1)} collective-permute-done((bf16[768,256]{1,0:T(8,128)(2,1)S(1)}, bf16[768,256]{1,0:T(8,128)(2,1)}, u32[]{:S(2)}, u32[]{:S(2)}) %collective-permute-start.2) | collective-permute-done | bytes 393248 | tf_op jit(solution)/shard_map/ppermute | solution.py:372
  15.5 8.8 %collective-permute-start.6 = (bf16[768,256]{1,0:T(8,128)(2,1)}, bf16[768,256]{1,0:T(8,128)(2,1)}, u32[]{:S(2)}, u32[]{:S(2)}) collective-permute-start(bf16[768,256]{1,0:T(8,128)(2,1)} %collective-permute-done.2.rest_3_), channel_id=1, source_target_pairs={{0,1},{1,0},{2,3},{3,2},{4,5},{5,4},{6,7},{7,6},{8,9},{9,8},{10,11... | collective-permute-start | bytes 1179656 | tf_op jit(solution)/shard_map/ppermute | solution.py:373
  24.3 3.3 %collective-permute-done.rest_1_ = bf16[768,256]{1,0:T(8,128)(2,1)} collective-permute-done((bf16[768,256]{1,0:T(8,128)(2,1)S(1)}, bf16[768,256]{1,0:T(8,128)(2,1)}, u32[]{:S(2)}, u32[]{:S(2)}) %collective-permute-start) | collective-permute-done | bytes 393248 | tf_op jit(solution)/shard_map/ppermute | solution.py:372
  30.8 2.6 %shard_map.127 = (bf16[2048,128]{1,0:T(8,128)(2,1)S(1)}, bf16[128,2048]{1,0:T(8,128)(2,1)S(1)}) custom-call(s32[8,128]{1,0:T(8,128)S(1)} %tile.13.columns_ref, s32[128,8]{1,0:T(8,128)S(1)} %bitcast.16, f32[128,8]{1,0:T(8,128)S(1)} %bitcast.15), custom_call_target="tpu_custom_call" | custom-call | tf_op jit(solution)/shard_map/pallas_call | solution.py:232
  33.6 2.2 %copy-done = bf16[512,4096]{1,0:T(8,128)(2,1)S(1)} copy-done((bf16[512,4096]{1,0:T(8,128)(2,1)S(1)}, bf16[512,4096]{1,0:T(8,128)(2,1)}, u32[]{:S(2)}) %copy-start) | copy-done | bytes 4194328
  36.7 13.1 %shard_map.129 = (bf16[4,16,2048]{2,1,0:T(8,128)(2,1)S(1)}, bf16[4,16,2048]{2,1,0:T(8,128)(2,1)S(1)}, bf16[4,16,2048]{2,1,0:T(8,128)(2,1)S(1)}, bf16[4,16,2048]{...) custom-call(s32[5]{0:T(128)S(1)} %stack.19.place_ref, ...), custom_call_target="tpu_custom_call" | custom-call | tf_op jit(solution)/shard_map/pallas_call | solution.py:160
  49.8 1.4 collective-permute-start.7
  51.2 2.6 %collective-permute-start.8 = (bf16[4,16,2048]{2,1,0:T(8,128)(2,1)S(1)}, bf16[4,16,2048]{2,1,0:T(8,128)(2,1)S(1)}, u32[]{:S(2)}, u32[]{:S(2)}) collective-permute-start(bf16[4,16,2048]{2,1,0:T(8,128)(2,1)S(1)} %get-tuple-element.33), channel_id=1, source_target_pairs={{0,16},{8,24},{16,0},{24,8},{1,17},{9,25},{17,1},{25,9},{2,18},{10... | collective-permute-start | bytes 786440 | tf_op jit(solution)/shard_map/ppermute | solution.py:377
  54.9 1.6 collective-permute-start.10
  56.5 3.3 %collective-permute-start.11 = (bf16[4,16,2048]{2,1,0:T(8,128)(2,1)S(1)}, bf16[4,16,2048]{2,1,0:T(8,128)(2,1)S(1)}, u32[]{:S(2)}, u32[]{:S(2)}) collective-permute-start(bf16[4,16,2048]{2,1,0:T(8,128)(2,1)S(1)} %get-tuple-element.37), channel_id=1, source_target_pairs={{0,64},{32,96},{64,0},{96,32},{1,65},{33,97},{65,1},{97,33},{2,66}... | collective-permute-start | bytes 786440 | tf_op jit(solution)/shard_map/ppermute | solution.py:378
  59.8 2.9 %collective-permute-start.12 = (bf16[4,16,2048]{2,1,0:T(8,128)(2,1)S(1)}, bf16[4,16,2048]{2,1,0:T(8,128)(2,1)S(1)}, u32[]{:S(2)}, u32[]{:S(2)}) collective-permute-start(bf16[4,16,2048]{2,1,0:T(8,128)(2,1)S(1)} %get-tuple-element.38), channel_id=1, source_target_pairs={{0,96},{32,0},{64,32},{96,64},{1,97},{33,1},{65,33},{97,65},{2,98}... | collective-permute-start | bytes 786440 | tf_op jit(solution)/shard_map/ppermute | solution.py:378
  62.7 3.2 %collective-permute-done.8.refs_2_ = bf16[4,16,2048]{2,1,0:T(8,128)(2,1)S(1)} collective-permute-done((bf16[4,16,2048]{2,1,0:T(8,128)(2,1)S(1)}, bf16[4,16,2048]{2,1,0:T(8,128)(2,1)S(1)}, u32[]{:S(2)}, u32[]{:S(2)}) %collective-permute-start.8) | collective-permute-done | bytes 262176 | tf_op jit(solution)/shard_map/ppermute | solution.py:377
  65.9 5.8 %collective-permute-done.11.refs_6_ = bf16[4,16,2048]{2,1,0:T(8,128)(2,1)S(1)} collective-permute-done((bf16[4,16,2048]{2,1,0:T(8,128)(2,1)S(1)}, bf16[4,16,2048]{2,1,0:T(8,128)(2,1)S(1)}, u32[]{:S(2)}, u32[]{:S(2)}) %collective-permute-start.11) | collective-permute-done | bytes 262176 | tf_op jit(solution)/shard_map/ppermute | solution.py:378
  72.6 2.1 %collective-permute-start.13 = (bf16[16,2048]{1,0:T(8,128)(2,1)S(1)}, bf16[16,2048]{1,0:T(8,128)(2,1)S(1)}, u32[]{:S(2)}, u32[]{:S(2)}) collective-permute-start(bf16[16,2048]{1,0:T(8,128)(2,1)S(1)} %get-tuple-element.40), channel_id=1, source_target_pairs={{0,32},{32,64},{64,96},{96,0},{1,33},{33,65},{65,97},{97,1},{2,34}... | collective-permute-start | bytes 196616 | tf_op jit(solution)/shard_map/ppermute | solution.py:380
  74.6 1.7 collective-permute-start.14
  78.6 2.1 %collective-permute-start.18 = (bf16[16,2048]{1,0:T(8,128)(2,1)S(1)}, bf16[16,2048]{1,0:T(8,128)(2,1)S(1)}, u32[]{:S(2)}, u32[]{:S(2)}) collective-permute-start(bf16[16,2048]{1,0:T(8,128)(2,1)S(1)} %get-tuple-element.46), channel_id=1, source_target_pairs={{0,24},{8,0},{16,8},{24,16},{1,25},{9,1},{17,9},{25,17},{2,26},{10... | collective-permute-start | bytes 196616 | tf_op jit(solution)/shard_map/ppermute | solution.py:381
  81.4 1.2 collective-permute-done.17.refs_6_
  83.6 41.5 %all_to_all.10.lines_ref = bf16[128,16,512]{2,1,0:T(8,128)(2,1)S(1)} all-to-all(bf16[128,16,512]{2,1,0:T(8,128)(2,1)S(1)} %get-tuple-element.48), channel_id=1, replica_groups=mesh['z'=4,'y'=4,'x'=4,'c'=2] {'z','y','x','c'}, dimensions={0} | all-to-all | bytes 4194304 | tf_op jit(solution)/shard_map/all_to_all | solution.py:386
  125.2 10.8 %shard_map.132 = bf16[128,16,512]{2,1,0:T(8,128)(2,1)S(1)} custom-call(bf16[128,16,512]{2,1,0:T(8,128)(2,1)S(1)} %all_to_all.10.lines_ref, bf16[4096,1536]{1,0:T(8,128)(2,1)} %bitcast.20, bf16[768,4096]{1,0:T(8,128)(2,1)S(1)} %bitcast.14), custom_call_target="tpu_custom_call" | custom-call | tf_op jit(solution)/shard_map/pallas_call | solution.py:319
  136.0 34.4 %all_to_all.11.lines_ref = bf16[128,16,512]{2,1,0:T(8,128)(2,1)S(1)} all-to-all(bf16[128,16,512]{2,1,0:T(8,128)(2,1)S(1)} %shard_map.132), channel_id=1, replica_groups=mesh['z'=4,'y'=4,'x'=4,'c'=2] {'z','y','x','c'}, dimensions={0} | all-to-all | bytes 4194304 | tf_op jit(solution)/shard_map/all_to_all | solution.py:388
  170.4 1.1 shard_map.133
  (56 shorter events, 12.6 us)
Async XLA Ops:
  0.0 33.5 %copy-start.7 = (f32[128]{0:T(128)S(1)}, f32[128]{0:T(128)}, u32[]{:S(2)}) copy-start(f32[128]{0:T(128)} %param.16) | copy-start | bytes 1540
  3.1 12.4 %collective-permute-start.2 = (bf16[768,256]{1,0:T(8,128)(2,1)S(1)}, bf16[768,256]{1,0:T(8,128)(2,1)}, u32[]{:S(2)}, u32[]{:S(2)}) collective-permute-start(bf16[768,256]{1,0:T(8,128)(2,1)S(1)} %shard_map.128.rest_0_), channel_id=1, source_target_pairs={{0,6},{2,0},{4,2},{6,4},{1,7},{3,1},{5,3},{7,5},{8,14},{10,8},{12,... | collective-permute-start | bytes 1179656 | tf_op jit(solution)/shard_map/ppermute | solution.py:372
  6.5 17.8 %collective-permute-start.1 = (bf16[768,256]{1,0:T(8,128)(2,1)S(1)}, bf16[768,256]{1,0:T(8,128)(2,1)}, u32[]{:S(2)}, u32[]{:S(2)}) collective-permute-start(bf16[768,256]{1,0:T(8,128)(2,1)S(1)} %shard_map.128.rest_0_), channel_id=1, source_target_pairs={{0,4},{2,6},{4,0},{6,2},{1,5},{3,7},{5,1},{7,3},{8,12},{10,14},{12... | collective-permute-start | bytes 1179656 | tf_op jit(solution)/shard_map/ppermute | solution.py:372
  7.0 20.6 %collective-permute-start = (bf16[768,256]{1,0:T(8,128)(2,1)S(1)}, bf16[768,256]{1,0:T(8,128)(2,1)}, u32[]{:S(2)}, u32[]{:S(2)}) collective-permute-start(bf16[768,256]{1,0:T(8,128)(2,1)S(1)} %shard_map.128.rest_0_), channel_id=1, source_target_pairs={{0,2},{2,4},{4,6},{6,0},{1,3},{3,5},{5,7},{7,1},{8,10},{10,12},{12... | collective-permute-start | bytes 1179656 | tf_op jit(solution)/shard_map/ppermute | solution.py:372
  7.6 25.9 %collective-permute-start.3 = (bf16[768,256]{1,0:T(8,128)(2,1)S(1)}, bf16[768,256]{1,0:T(8,128)(2,1)}, u32[]{:S(2)}, u32[]{:S(2)}) collective-permute-start(bf16[768,256]{1,0:T(8,128)(2,1)S(1)} %shard_map.128.rest_0_), channel_id=1, source_target_pairs={{0,1},{1,0},{2,3},{3,2},{4,5},{5,4},{6,7},{7,6},{8,9},{9,8},{10,11... | collective-permute-start | bytes 1179656 | tf_op jit(solution)/shard_map/ppermute | solution.py:373
  15.5 18.0 %collective-permute-start.6 = (bf16[768,256]{1,0:T(8,128)(2,1)}, bf16[768,256]{1,0:T(8,128)(2,1)}, u32[]{:S(2)}, u32[]{:S(2)}) collective-permute-start(bf16[768,256]{1,0:T(8,128)(2,1)} %collective-permute-done.2.rest_3_), channel_id=1, source_target_pairs={{0,1},{1,0},{2,3},{3,2},{4,5},{5,4},{6,7},{7,6},{8,9},{9,8},{10,11... | collective-permute-start | bytes 1179656 | tf_op jit(solution)/shard_map/ppermute | solution.py:373
  24.3 9.2 %collective-permute-start.5 = (bf16[768,256]{1,0:T(8,128)(2,1)}, bf16[768,256]{1,0:T(8,128)(2,1)}, u32[]{:S(2)}, u32[]{:S(2)}) collective-permute-start(bf16[768,256]{1,0:T(8,128)(2,1)} %collective-permute-done.1.rest_2_), channel_id=1, source_target_pairs={{0,1},{1,0},{2,3},{3,2},{4,5},{5,4},{6,7},{7,6},{8,9},{9,8},{10,11... | collective-permute-start | bytes 1179656 | tf_op jit(solution)/shard_map/ppermute | solution.py:373
  27.6 5.9 %collective-permute-start.4 = (bf16[768,256]{1,0:T(8,128)(2,1)}, bf16[768,256]{1,0:T(8,128)(2,1)}, u32[]{:S(2)}, u32[]{:S(2)}) collective-permute-start(bf16[768,256]{1,0:T(8,128)(2,1)} %collective-permute-done.rest_1_), channel_id=1, source_target_pairs={{0,1},{1,0},{2,3},{3,2},{4,5},{5,4},{6,7},{7,6},{8,9},{9,8},{10,11... | collective-permute-start | bytes 1179656 | tf_op jit(solution)/shard_map/ppermute | solution.py:373
  30.8 94.4 %slice-start = ((s8[6291456]{0:T(1024)(128)(4,1)}), s8[2097152]{0:T(1024)(128)(4,1)S(1)}, s32[]{:S(2)}) async-start(s8[6291456]{0:T(1024)(128)(4,1)} %bitcast.12), calls=%async_computation.2 | async-start | bytes 4194304
  36.7 88.5 %slice-start.1 = ((s8[6291456]{0:T(1024)(128)(4,1)}), s8[4194304]{0:T(1024)(128)(4,1)S(1)}, s32[]{:S(2)}) async-start(s8[6291456]{0:T(1024)(128)(4,1)} %bitcast.12), calls=%async_computation.3 | async-start | bytes 8388608
  49.8 33.0 %copy-start.4 = (bf16[16,4096]{1,0:T(8,128)(2,1)S(1)}, bf16[16,4096]{1,0:T(8,128)(2,1)}, u32[]{:S(2)}) copy-start(bf16[16,4096]{1,0:T(8,128)(2,1)} %refs_8_.1) | copy-start | bytes 393220
  49.8 32.9 %copy-start.5 = (f32[4096]{0:T(1024)S(1)}, f32[4096]{0:T(1024)}, u32[]{:S(2)}) copy-start(f32[4096]{0:T(1024)} %param.20) | copy-start | bytes 49156
  49.8 10.0 %collective-permute-start.7 = (bf16[4,16,2048]{2,1,0:T(8,128)(2,1)S(1)}, bf16[4,16,2048]{2,1,0:T(8,128)(2,1)S(1)}, u32[]{:S(2)}, u32[]{:S(2)}) collective-permute-start(bf16[4,16,2048]{2,1,0:T(8,128)(2,1)S(1)} %get-tuple-element.32), channel_id=1, source_target_pairs={{0,8},{8,16},{16,24},{24,0},{1,9},{9,17},{17,25},{25,1},{2,10},{10... | collective-permute-start | bytes 786440 | tf_op jit(solution)/shard_map/ppermute | solution.py:377
  51.2 14.7 %collective-permute-start.8 = (bf16[4,16,2048]{2,1,0:T(8,128)(2,1)S(1)}, bf16[4,16,2048]{2,1,0:T(8,128)(2,1)S(1)}, u32[]{:S(2)}, u32[]{:S(2)}) collective-permute-start(bf16[4,16,2048]{2,1,0:T(8,128)(2,1)S(1)} %get-tuple-element.33), channel_id=1, source_target_pairs={{0,16},{8,24},{16,0},{24,8},{1,17},{9,25},{17,1},{25,9},{2,18},{10... | collective-permute-start | bytes 786440 | tf_op jit(solution)/shard_map/ppermute | solution.py:377
  53.8 12.1 %collective-permute-start.9 = (bf16[4,16,2048]{2,1,0:T(8,128)(2,1)S(1)}, bf16[4,16,2048]{2,1,0:T(8,128)(2,1)S(1)}, u32[]{:S(2)}, u32[]{:S(2)}) collective-permute-start(bf16[4,16,2048]{2,1,0:T(8,128)(2,1)S(1)} %get-tuple-element.34), channel_id=1, source_target_pairs={{0,24},{8,0},{16,8},{24,16},{1,25},{9,1},{17,9},{25,17},{2,26},{10... | collective-permute-start | bytes 786440 | tf_op jit(solution)/shard_map/ppermute | solution.py:377
  54.9 11.0 %collective-permute-start.10 = (bf16[4,16,2048]{2,1,0:T(8,128)(2,1)S(1)}, bf16[4,16,2048]{2,1,0:T(8,128)(2,1)S(1)}, u32[]{:S(2)}, u32[]{:S(2)}) collective-permute-start(bf16[4,16,2048]{2,1,0:T(8,128)(2,1)S(1)} %get-tuple-element.36), channel_id=1, source_target_pairs={{0,32},{32,64},{64,96},{96,0},{1,33},{33,65},{65,97},{97,1},{2,34}... | collective-permute-start | bytes 786440 | tf_op jit(solution)/shard_map/ppermute | solution.py:378
  56.5 15.2 %collective-permute-start.11 = (bf16[4,16,2048]{2,1,0:T(8,128)(2,1)S(1)}, bf16[4,16,2048]{2,1,0:T(8,128)(2,1)S(1)}, u32[]{:S(2)}, u32[]{:S(2)}) collective-permute-start(bf16[4,16,2048]{2,1,0:T(8,128)(2,1)S(1)} %get-tuple-element.37), channel_id=1, source_target_pairs={{0,64},{32,96},{64,0},{96,32},{1,65},{33,97},{65,1},{97,33},{2,66}... | collective-permute-start | bytes 786440 | tf_op jit(solution)/shard_map/ppermute | solution.py:378
  59.8 11.9 %collective-permute-start.12 = (bf16[4,16,2048]{2,1,0:T(8,128)(2,1)S(1)}, bf16[4,16,2048]{2,1,0:T(8,128)(2,1)S(1)}, u32[]{:S(2)}, u32[]{:S(2)}) collective-permute-start(bf16[4,16,2048]{2,1,0:T(8,128)(2,1)S(1)} %get-tuple-element.38), channel_id=1, source_target_pairs={{0,96},{32,0},{64,32},{96,64},{1,97},{33,1},{65,33},{97,65},{2,98}... | collective-permute-start | bytes 786440 | tf_op jit(solution)/shard_map/ppermute | solution.py:378
  72.6 6.0 %collective-permute-start.13 = (bf16[16,2048]{1,0:T(8,128)(2,1)S(1)}, bf16[16,2048]{1,0:T(8,128)(2,1)S(1)}, u32[]{:S(2)}, u32[]{:S(2)}) collective-permute-start(bf16[16,2048]{1,0:T(8,128)(2,1)S(1)} %get-tuple-element.40), channel_id=1, source_target_pairs={{0,32},{32,64},{64,96},{96,0},{1,33},{33,65},{65,97},{97,1},{2,34}... | collective-permute-start | bytes 196616 | tf_op jit(solution)/shard_map/ppermute | solution.py:380
  74.6 6.0 %collective-permute-start.14 = (bf16[16,2048]{1,0:T(8,128)(2,1)S(1)}, bf16[16,2048]{1,0:T(8,128)(2,1)S(1)}, u32[]{:S(2)}, u32[]{:S(2)}) collective-permute-start(bf16[16,2048]{1,0:T(8,128)(2,1)S(1)} %get-tuple-element.41), channel_id=1, source_target_pairs={{0,64},{32,96},{64,0},{96,32},{1,65},{33,97},{65,1},{97,33},{2,66}... | collective-permute-start | bytes 196616 | tf_op jit(solution)/shard_map/ppermute | solution.py:380
  76.3 4.3 %collective-permute-start.15 = (bf16[16,2048]{1,0:T(8,128)(2,1)S(1)}, bf16[16,2048]{1,0:T(8,128)(2,1)S(1)}, u32[]{:S(2)}, u32[]{:S(2)}) collective-permute-start(bf16[16,2048]{1,0:T(8,128)(2,1)S(1)} %get-tuple-element.42), channel_id=1, source_target_pairs={{0,96},{32,0},{64,32},{96,64},{1,97},{33,1},{65,33},{97,65},{2,98}... | collective-permute-start | bytes 196616 | tf_op jit(solution)/shard_map/ppermute | solution.py:380
  77.1 4.3 %collective-permute-start.16 = (bf16[16,2048]{1,0:T(8,128)(2,1)S(1)}, bf16[16,2048]{1,0:T(8,128)(2,1)S(1)}, u32[]{:S(2)}, u32[]{:S(2)}) collective-permute-start(bf16[16,2048]{1,0:T(8,128)(2,1)S(1)} %get-tuple-element.44), channel_id=1, source_target_pairs={{0,8},{8,16},{16,24},{24,0},{1,9},{9,17},{17,25},{25,1},{2,10},{10... | collective-permute-start | bytes 196616 | tf_op jit(solution)/shard_map/ppermute | solution.py:381
  77.6 5.1 %collective-permute-start.17 = (bf16[16,2048]{1,0:T(8,128)(2,1)S(1)}, bf16[16,2048]{1,0:T(8,128)(2,1)S(1)}, u32[]{:S(2)}, u32[]{:S(2)}) collective-permute-start(bf16[16,2048]{1,0:T(8,128)(2,1)S(1)} %get-tuple-element.45), channel_id=1, source_target_pairs={{0,16},{8,24},{16,0},{24,8},{1,17},{9,25},{17,1},{25,9},{2,18},{10... | collective-permute-start | bytes 196616 | tf_op jit(solution)/shard_map/ppermute | solution.py:381
  78.6 4.2 %collective-permute-start.18 = (bf16[16,2048]{1,0:T(8,128)(2,1)S(1)}, bf16[16,2048]{1,0:T(8,128)(2,1)S(1)}, u32[]{:S(2)}, u32[]{:S(2)}) collective-permute-start(bf16[16,2048]{1,0:T(8,128)(2,1)S(1)} %get-tuple-element.46), channel_id=1, source_target_pairs={{0,24},{8,0},{16,8},{24,16},{1,25},{9,1},{17,9},{25,17},{2,26},{10... | collective-permute-start | bytes 196616 | tf_op jit(solution)/shard_map/ppermute | solution.py:381
  (5 other events, 6.1 us)

commit v2 on v1

v2 whole, which is shorter than its diff:
```python
import functools
import math

import jax
import jax.numpy as jnp
from jax import lax
from jax.experimental import pallas as pl
from jax.experimental.pallas import tpu as pltpu
from jax.sharding import Mesh
from jax.sharding import PartitionSpec as P

HEADS = 64
KV_HEADS = 4
HD = 128
WIDTH = 4096
ROWS = 16
QROWS = 256
QHEADS = 4
CACHE_ROWS = 512
SHARD = CACHE_ROWS + QROWS
GROUPS = 16
EXPERTS = 128
SLOTS = 2
CHUNKS = 8
PIECE = WIDTH // CHUNKS
LINES = CHUNKS * SLOTS
FFE = 768
GROUP = 16
GROUP_LINES = GROUP * LINES
EPSILON = 1e-06
SCALE = math.log2(math.e) / math.sqrt(HD)
MB = 1 << 20

F32 = jnp.float32
BF16 = jnp.bfloat16

VMEM = functools.partial(pl.BlockSpec, memory_space=pltpu.VMEM)
SMEM = functools.partial(pl.BlockSpec, memory_space=pltpu.SMEM)
HBM = functools.partial(pl.BlockSpec, memory_space=pltpu.HBM)


def params(limit):
    return pltpu.CompilerParams(vmem_limit_bytes=limit * MB)


def rms_scale(values, gain):
    mean_square = jnp.mean(values * values, axis=-1, keepdims=True)
    return values * lax.rsqrt(mean_square + EPSILON) * gain


def shift(step):
    return [(i, (i + step) % 4) for i in range(4)]


def prep_kernel(place_ref, cache_ref, new_ref, gain_ref, out_ref, cache, new, sems):
    head = place_ref[1]
    copies = (
        pltpu.make_async_copy(cache_ref.at[head], cache, sems.at[0]),
        pltpu.make_async_copy(new_ref.at[head], new, sems.at[1]),
    )
    for copy in copies:
        copy.start()
    for copy, ref, start, rows in (
        (copies[1], new, CACHE_ROWS, QROWS),
        (copies[0], cache, 0, CACHE_ROWS),
    ):
        copy.wait()
        keys = rms_scale(ref[:, :HD].astype(F32), gain_ref[...]).astype(BF16)
        out_ref[pl.ds(start, rows), :HD] = keys
        out_ref[pl.ds(start, rows), HD:] = ref[:, HD:]


def prep(place, cache, new_kv, k_gain):
    return pl.pallas_call(
        prep_kernel,
        in_specs=[SMEM(), HBM(), HBM(), VMEM()],
        out_specs=VMEM(),
        out_shape=jax.ShapeDtypeStruct((SHARD, 2 * HD), BF16),
        scratch_shapes=[
            pltpu.VMEM((CACHE_ROWS, 2 * HD), BF16),
            pltpu.VMEM((QROWS, 2 * HD), BF16),
            pltpu.SemaphoreType.DMA((2,)),
        ],
        compiler_params=params(8),
    )(place, cache, new_kv, k_gain)


def seen_blocks(place_ref, core_offset, distances, shards, qn, acc, total):
    limit, x, c = place_ref[0], place_ref[3], place_ref[4]
    core = lax.rem(c + core_offset, 2)
    tok = x * 2 + c

    def block(ref, start, rows, mask):
        keys = ref[pl.ds(start, rows), :HD]
        values = ref[pl.ds(start, rows), HD:]
        scores = lax.dot_general(
            qn[...], keys, (((1,), (1,)), ((), ())), preferred_element_type=F32
        )
        weights = jnp.exp2(scores * SCALE)
        if mask is not None:
            weights = jnp.where(mask, weights, 0.0)
        part = weights[:, :HD]
        for i in range(1, rows // HD):
            part = part + weights[:, i * HD : (i + 1) * HD]
        total[...] += part
        acc[...] += jnp.dot(weights.astype(BF16), values, preferred_element_type=F32)

    for distance, ref in zip(distances, shards):
        owner = lax.rem(x + 4 - distance, 4) * 2 + core
        visible = limit - owner * CACHE_ROWS

        @pl.when(visible >= CACHE_ROWS)
        def _():
            block(ref, 0, CACHE_ROWS, None)

        @pl.when((visible > 0) & (visible < CACHE_ROWS))
        def _():
            key = lax.broadcasted_iota(jnp.int32, (QHEADS * QROWS, CACHE_ROWS), 1)
            block(ref, 0, CACHE_ROWS, key < visible)

        if distance == 0 and core_offset == 0:
            key = lax.broadcasted_iota(jnp.int32, (QHEADS * QROWS, QROWS), 1)
            query = lax.broadcasted_iota(jnp.int32, (QHEADS * QROWS, QROWS), 0)
            block(ref, CACHE_ROWS, QROWS, key <= lax.rem(query, QROWS))
        else:

            @pl.when(owner < tok)
            def _():
                block(ref, CACHE_ROWS, QROWS, None)


def near_kernel(place_ref, q_ref, gain_ref, own_ref, other_ref, qn, acc, total):
    for h in range(QHEADS):
        head = q_ref[:, h * HD : (h + 1) * HD].astype(F32)
        qn[pl.ds(h * QROWS, QROWS), :] = rms_scale(head, gain_ref[...]).astype(BF16)
    acc[...] = jnp.zeros_like(acc)
    total[...] = jnp.zeros_like(total)
    seen_blocks(place_ref, 0, (0,), (own_ref,), qn, acc, total)
    seen_blocks(place_ref, 1, (0,), (other_ref,), qn, acc, total)


STATE = (
    jax.ShapeDtypeStruct((QHEADS * QROWS, HD), F32),
    jax.ShapeDtypeStruct((QHEADS * QROWS, HD), F32),
)


def attend_near(place, queries, q_gain, own, other):
    return pl.pallas_call(
        near_kernel,
        in_specs=[SMEM()] + [VMEM()] * 4,
        out_specs=[VMEM()] * 3,
        out_shape=[jax.ShapeDtypeStruct((QHEADS * QROWS, HD), BF16), *STATE],
        compiler_params=params(16),
    )(place, queries, q_gain, own, other)


def far_kernel(place_ref, qn, acc_ref, total_ref, first, second, third, acc, total):
    acc[...] = acc_ref[...]
    total[...] = total_ref[...]
    seen_blocks(place_ref, 0, (1, 2, 3), (first, second, third), qn, acc, total)


def attend_far(place, qn, acc, total, shards):
    return pl.pallas_call(
        far_kernel,
        in_specs=[SMEM()] + [VMEM()] * 6,
        out_specs=[VMEM()] * 2,
        out_shape=list(STATE),
        compiler_params=params(16),
    )(place, qn, acc, total, *shards)


def last_kernel(
    place_ref, qn, acc_ref, total_ref, first, second, third, weight_ref, out_ref, acc, total, attn,
    weight, sem,
):
    copy = pltpu.make_async_copy(weight_ref, weight, sem)
    copy.start()
    acc[...] = acc_ref[...]
    total[...] = total_ref[...]
    seen_blocks(place_ref, 1, (1, 2, 3), (first, second, third), qn, acc, total)
    for h in range(QHEADS):
        at = pl.ds(h * QROWS, QROWS)
        whole = jnp.sum(total[at, :], axis=1, keepdims=True)
        attn[:, h * HD : (h + 1) * HD] = (acc[at, :] / whole).astype(BF16)
    copy.wait()
    for n in range(8):
        columns = slice(n * 512, (n + 1) * 512)
        product = jnp.dot(attn[...], weight[:, columns], preferred_element_type=F32)
        out_ref[:, :, columns] = product.astype(BF16).reshape(GROUPS, ROWS, 512)


def attend_last(place, qn, acc, total, shards, weight):
    return pl.pallas_call(
        last_kernel,
        in_specs=[SMEM()] + [VMEM()] * 6 + [HBM()],
        out_specs=VMEM(),
        out_shape=jax.ShapeDtypeStruct((GROUPS, ROWS, WIDTH), BF16),
        scratch_shapes=[
            pltpu.VMEM((QHEADS * QROWS, HD), F32),
            pltpu.VMEM((QHEADS * QROWS, HD), F32),
            pltpu.VMEM((QROWS, QHEADS * HD), BF16),
            pltpu.VMEM((QHEADS * HD, WIDTH), BF16),
            pltpu.SemaphoreType.DMA,
        ],
        compiler_params=params(20),
    )(place, qn, acc, total, *shards, weight)


def route_kernel(columns_ref, rows_ref, mix_ref, placing_ref, mixing_ref):
    line = lax.broadcasted_iota(jnp.int32, (EXPERTS * LINES, EXPERTS), 0)
    lane = lax.broadcasted_iota(jnp.int32, (EXPERTS * LINES, EXPERTS), 1)
    slot = (line // LINES) * SLOTS + line % SLOTS
    hit = slot == columns_ref[0:1, :]
    for k in range(1, 8):
        hit = hit | (slot == columns_ref[k : k + 1, :])
    hit = hit & ((line // SLOTS) % CHUNKS == lane // ROWS)
    placing_ref[...] = jnp.where(hit, 1.0, 0.0).astype(BF16)
    line = lax.broadcasted_iota(jnp.int32, (EXPERTS, EXPERTS * LINES), 1)
    row = lax.broadcasted_iota(jnp.int32, (EXPERTS, EXPERTS * LINES), 0)
    slot = (line // LINES) * SLOTS + line % SLOTS
    value = jnp.zeros(slot.shape, F32)
    for k in range(8):
        value = jnp.where(slot == rows_ref[:, k : k + 1], mix_ref[:, k : k + 1], value)
    same = (line // SLOTS) % CHUNKS == row // ROWS
    mixing_ref[...] = jnp.where(same, value, 0.0).astype(BF16)


def route(expert_ids, combine_weight):
    flat = expert_ids.reshape(-1)
    index = jnp.arange(flat.shape[0], dtype=jnp.int32)
    earlier = (flat[:, None] == flat[None, :]) & (index[None, :] < index[:, None])
    slot = jnp.sum(earlier.astype(jnp.int32), axis=1)
    target = (flat * SLOTS + slot).reshape(expert_ids.shape)
    return pl.pallas_call(
        route_kernel,
        in_specs=[VMEM()] * 3,
        out_specs=[VMEM()] * 2,
        out_shape=[
            jax.ShapeDtypeStruct((EXPERTS * LINES, EXPERTS), BF16),
            jax.ShapeDtypeStruct((EXPERTS, EXPERTS * LINES), BF16),
        ],
        compiler_params=params(12),
    )(
        jnp.tile(target.T, (1, CHUNKS)),
        jnp.tile(target, (CHUNKS, 1)),
        jnp.tile(combine_weight.astype(F32), (CHUNKS, 1)),
    )


def dispatch_kernel(parts_ref, residual_ref, gain_ref, placing_ref, hidden_ref, out_ref, pieces):
    for n in range(8):
        columns = slice(n * 512, (n + 1) * 512)
        value = residual_ref[:, columns].astype(F32)
        for g in range(GROUPS):
            value = value + parts_ref[g, :, columns].astype(F32)
        hidden_ref[:, columns] = value
    normed = rms_scale(hidden_ref[...], gain_ref[...]).astype(BF16)
    for k in range(CHUNKS):
        pieces[pl.ds(k * ROWS, ROWS), :] = normed[:, k * PIECE : (k + 1) * PIECE]
    for g in range(8):
        lines = jnp.dot(
            placing_ref[pl.ds(g * GROUP_LINES, GROUP_LINES), :],
            pieces[...],
            preferred_element_type=F32,
        )
        out_ref[pl.ds(g * GROUP, GROUP)] = lines.astype(BF16).reshape(GROUP, LINES, PIECE)


def dispatch(parts, residual, norm_gain, placing):
    return pl.pallas_call(
        dispatch_kernel,
        in_specs=[VMEM()] * 4,
        out_specs=[VMEM()] * 2,
        out_shape=[
            jax.ShapeDtypeStruct((ROWS, WIDTH), F32),
            jax.ShapeDtypeStruct((EXPERTS, LINES, PIECE), BF16),
        ],
        scratch_shapes=[pltpu.VMEM((EXPERTS, PIECE), BF16)],
        compiler_params=params(12),
    )(parts, residual, norm_gain, placing)


def expert_kernel(
    lines_ref, up_ref, down_hbm, out_ref, rows, both, active, back, down_ref, sem
):
    copy = pltpu.make_async_copy(down_hbm, down_ref, sem)
    copy.start()
    size = (GROUP_LINES, GROUP_LINES)
    first = lax.broadcasted_iota(jnp.int32, size, 0)
    second = lax.broadcasted_iota(jnp.int32, size, 1)
    span = GROUP * SLOTS

    def held(by_chunk, by_source):
        source = (by_chunk % span) // SLOTS
        line = source * LINES + (by_chunk // span) * SLOTS + by_chunk % SLOTS
        return jnp.where(line == by_source, 1.0, 0.0).astype(BF16)

    gather, scatter = held(first, second), held(second, first)
    for g in range(8):
        group = lines_ref[pl.ds(g * GROUP, GROUP)].reshape(GROUP_LINES, PIECE)
        sorted_lines = jnp.dot(gather, group, preferred_element_type=F32).astype(BF16)
        for k in range(CHUNKS):
            rows[pl.ds(g * span, span), k * PIECE : (k + 1) * PIECE] = sorted_lines[
                k * span : (k + 1) * span, :
            ]
    for n in range(2 * FFE // 256):
        columns = slice(n * 256, (n + 1) * 256)
        both[:, columns] = jnp.dot(rows[...], up_ref[:, columns], preferred_element_type=F32)
    gate = both[:, :FFE]
    active[...] = (gate * jax.nn.sigmoid(gate) * both[:, FFE:]).astype(BF16)
    copy.wait()
    for k in range(CHUNKS):
        columns = slice(k * PIECE, (k + 1) * PIECE)
        down = jnp.dot(active[...], down_ref[:, columns], preferred_element_type=F32)
        down = down.astype(BF16)
        for g in range(8):
            back[g, pl.ds(k * span, span), :] = down[g * span : (g + 1) * span, :]
    for g in range(8):
        lines = jnp.dot(scatter, back[g], preferred_element_type=F32).astype(BF16)
        out_ref[pl.ds(g * GROUP, GROUP)] = lines.reshape(GROUP, LINES, PIECE)


def experts(lines, gate_up, down):
    return pl.pallas_call(
        expert_kernel,
        in_specs=[VMEM(), VMEM(), HBM()],
        out_specs=VMEM(),
        out_shape=jax.ShapeDtypeStruct((EXPERTS, LINES, PIECE), BF16),
        scratch_shapes=[
            pltpu.VMEM((EXPERTS * SLOTS, WIDTH), BF16),
            pltpu.VMEM((EXPERTS * SLOTS, 2 * FFE), F32),
            pltpu.VMEM((EXPERTS * SLOTS, FFE), BF16),
            pltpu.VMEM((8, GROUP_LINES, PIECE), BF16),
            pltpu.VMEM((FFE, WIDTH), BF16),
            pltpu.SemaphoreType.DMA,
        ],
        compiler_params=params(24),
    )(lines, gate_up, down)


def combine_kernel(lines_ref, mixing_ref, hidden_ref, out_ref):
    lines = lines_ref[...].reshape(EXPERTS * LINES, PIECE)
    mixed = jnp.dot(mixing_ref[...], lines, preferred_element_type=F32)
    for k in range(CHUNKS):
        columns = slice(k * PIECE, (k + 1) * PIECE)
        value = hidden_ref[:, columns] + mixed[k * ROWS : (k + 1) * ROWS, :]
        out_ref[:, columns] = value.astype(BF16)


def combine(lines, mixing, hidden):
    return pl.pallas_call(
        combine_kernel,
        in_specs=[VMEM()] * 3,
        out_specs=VMEM(),
        out_shape=jax.ShapeDtypeStruct((ROWS, WIDTH), BF16),
        compiler_params=params(12),
    )(lines, mixing, hidden)


def per_device(
    queries,
    cache,
    new_kv,
    q_gain,
    k_gain,
    out_weight,
    residual,
    norm_gain,
    expert_ids,
    combine_weight,
    prefix_len,
    w_gate_up,
    w_down,
):
    z, y, x, c = (lax.axis_index(name).astype(jnp.int32) for name in ("z", "y", "x", "c"))
    place = jnp.stack([prefix_len[0], z, y, x, c])
    held = functools.partial(pltpu.with_memory_space_constraint, memory_space=pltpu.HBM)
    own = prep(place, held(cache), held(new_kv), k_gain.reshape(1, HD))
    swap = functools.partial(lax.ppermute, axis_name="c", perm=[(0, 1), (1, 0)])
    other = swap(own)
    near = [lax.ppermute(own, "x", shift(k)) for k in (1, 2, 3)]
    placing, mixing = route(expert_ids, combine_weight)
    queries, placing, mixing = lax.optimization_barrier((queries, placing, mixing))
    qn, acc, total = attend_near(place, queries, q_gain.reshape(1, HD), own, other)
    *near, qn, acc, total = lax.optimization_barrier((*near, qn, acc, total))
    far = [swap(shard) for shard in near]
    acc, total = attend_far(place, qn, acc, total, near)
    parts = attend_last(place, qn, acc, total, far, held(out_weight))
    parts = lax.all_to_all(parts, ("z", "y"), split_axis=0, concat_axis=0, tiled=True)
    hidden, lines = dispatch(parts, residual, norm_gain.reshape(1, WIDTH), placing)
    everyone = ("z", "y", "x", "c")
    lines = lax.all_to_all(lines, everyone, split_axis=0, concat_axis=0, tiled=True)
    lines = experts(lines, w_gate_up[0], w_down[0])
    lines = lax.all_to_all(lines, everyone, split_axis=0, concat_axis=0, tiled=True)
    return combine(lines, mixing, hidden)


def solution(mesh):
    fine = Mesh(mesh.devices.reshape(4, 4, 4, 2), ("z", "y", "x", "c"))
    head, tok = ("z", "y"), ("x", "c")
    placed = (
        P(tok, head),
        P(None, tok, None),
        P(None, tok, None),
        P(),
        P(),
        P(head, None),
        P(tok + head, None),
        P(),
        P(tok + head, None),
        P(tok + head, None),
        P(),
        P(head + tok, None, None),
        P(head + tok, None, None),
    )
    return jax.shard_map(
        per_device, mesh=fine, in_specs=placed, out_specs=P(tok + head, None), check_vma=False
    )
```

time: 172 us -> 155 us (0.901)
  blocking collectives: 75.9 us -> 109 us
  starting transfers between devices: 36.2 us -> 6.21 us
  waiting for transfers between devices: 20.8 us -> 4.66 us
  Pallas kernels: 29.5 us -> 24.1 us
    all_to_all x0 -> x1, blocking collectives: none -> 35.2 us  [per_device(): lax.all_to_all(parts, ('z', 'y'), split_axis=0, concat_axis=0, tiled=True)]
    ppermute x19 -> x7, starting transfers between devices: 36.2 us -> 6.21 us  [the longest x3 3.7 us: per_device(): near = [lax.ppermute(own, 'x', shift(k)) for k in (1, 2, 3)]]
    ppermute x19 -> x7, waiting for transfers between devices: 20.8 us -> 4.66 us  [the longest x3 4.65 us: per_device(): near = [lax.ppermute(own, 'x', shift(k)) for k in (1, 2, 3)]]
    pallas_call x5 -> x6, Pallas kernels: 25.8 us -> 20.4 us  [the longest x1 6.83 us: experts(): pl.pallas_call(expert_kernel, in_specs=[VMEM(), VMEM(), HBM()], out_specs...]
    unnamed x21, local copies, waits for them, and re-layouts: 6.85 us -> 2.06 us
    all_to_all x2, blocking collectives: 75.9 us -> 73.3 us  [per_device(): lax.all_to_all(lines, everyone, split_axis=0, concat_axis=0, tiled=True)]
  transfers between devices with their start and end apart: 19 -> 7, of which waited for: 7 -> 2; matrix products, arithmetic and copies ran while one was open for 1% -> 6% of each run, Pallas kernels for 2% -> 6%
where the time goes in v2:
time: 155 us; the launch traced here: 154 us
  blocking collectives  109 us (70%)
  Pallas kernels  24.1 us (16%)
  local copies, waits for them, and re-layouts  8.58 us (6%)
  starting transfers between devices  6.21 us (4%)
  waiting for transfers between devices  4.66 us (3%)
    all_to_all x2, blocking collectives, per_device(): lax.all_to_all(lines, everyone, split_axis=0, concat_axis=0, tiled=True)  73.3 us
    all_to_all x1, blocking collectives, per_device(): lax.all_to_all(parts, ('z', 'y'), split_axis=0, concat_axis=0, tiled=True)  35.2 us
    pallas_call x1, Pallas kernels, experts(): pl.pallas_call(expert_kernel, in_specs=[VMEM(), VMEM(), HBM()], out_specs...  6.83 us
    ppermute x3, waiting for transfers between devices, per_device(): near = [lax.ppermute(own, 'x', shift(k)) for k in (1, 2, 3)]  4.65 us
    pallas_call x1, Pallas kernels, attend_last(): pl.pallas_call(last_kernel, in_specs=[SMEM()] + [VMEM()] * 6 + [HBM()], o...  4.32 us
    ppermute x3, starting transfers between devices, per_device(): near = [lax.ppermute(own, 'x', shift(k)) for k in (1, 2, 3)]  3.7 us
    pallas_call x1, Pallas kernels, attend_near(): pl.pallas_call(near_kernel, in_specs=[SMEM()] + [VMEM()] * 4, out_specs=[...  3.37 us
  transfers between devices with their start and end apart: 7, of which 2 were waited for; matrix products, arithmetic and copies ran while one was open for 6% of the time, Pallas kernels for 6%

profile of v2, /device:TPU:1, one launch (start us, length us, event | category | flops | bytes accessed | tf_op | source)
XLA Modules:
  0.0 154.5 jit_solution(7322607385149897102)
XLA Ops:
  0.8 0.7 copy-done.4
  1.4 1.9 %shard_map.127.own_ref = bf16[768,256]{1,0:T(8,128)(2,1)S(1)} custom-call(s32[5]{0:T(128)S(1)} %stack.19.place_ref, bf16[4,512,256]{2,1,0:T(8,128)(2,1)} %cache_ref.1, bf16[4,256,256]{2,1,0:T(8,128)(2,1)} %new_ref.1, f32[1,128]{1,0:T(1,128)S(1)} %bitcast.22), custom_call_target="tpu_custom_call" | custom-call | tf_op jit(solution)/shard_map/pallas_call | solution.py:74
  3.4 1.5 collective-permute-start.3
  4.9 2.6 %collective-permute-start.2 = (bf16[768,256]{1,0:T(8,128)(2,1)S(1)}, bf16[768,256]{1,0:T(8,128)(2,1)S(1)}, u32[]{:S(2)}, u32[]{:S(2)}) collective-permute-start(bf16[768,256]{1,0:T(8,128)(2,1)S(1)} %shard_map.127.own_ref), channel_id=1, source_target_pairs={{0,6},{2,0},{4,2},{6,4},{1,7},{3,1},{5,3},{7,5},{8,14},{10,8},{12,... | collective-permute-start | bytes 1179656 | tf_op jit(solution)/shard_map/ppermute | solution.py:383
  8.6 1.4 copy.22
  9.9 0.8 eq.15
  10.9 0.7 reduce_sum.12
  11.6 1.3 multiply_add_fusion
  12.9 0.8 copy.24
  13.7 1.3 copy.25
  15.6 0.8 tile.13.columns_ref
  16.5 0.7 tile.30
  17.2 0.7 tile.28
  17.9 2.6 %shard_map.128 = (bf16[2048,128]{1,0:T(8,128)(2,1)S(1)}, bf16[128,2048]{1,0:T(8,128)(2,1)S(1)}) custom-call(s32[8,128]{1,0:T(8,128)S(1)} %tile.13.columns_ref, s32[128,8]{1,0:T(8,128)S(1)} %bitcast.19, f32[128,8]{1,0:T(8,128)S(1)} %bitcast.18), custom_call_target="tpu_custom_call" | custom-call | tf_op jit(solution)/shard_map/pallas_call | solution.py:236
  20.5 3.4 %shard_map.129 = (bf16[1024,128]{1,0:T(8,128)(2,1)S(1)}, f32[1024,128]{1,0:T(8,128)S(1)}, f32[1024,128]{1,0:T(8,128)S(1)}) custom-call(s32[5]{0:T(128)S(1)} %stack.19.place_ref, bf16[256,512]{1,0:T(8,128)(2,1)S(1)} %copy-done, f32[1,128]{1,0:T(1,128)S(1)} %bitcast.21, bf16[768,256]{1,0:T(8,128)(2,1)S(1)} %shard_map.127.own_ref, ...), custom_call_target="tpu_custom_call" | custom-call | tf_op jit(solution)/shard_map/pallas_call | solution.py:149
  24.2 4.3 %collective-permute-done.first = bf16[768,256]{1,0:T(8,128)(2,1)} collective-permute-done((bf16[768,256]{1,0:T(8,128)(2,1)S(1)}, bf16[768,256]{1,0:T(8,128)(2,1)}, u32[]{:S(2)}, u32[]{:S(2)}) %collective-permute-start) | collective-permute-done | bytes 393248 | tf_op jit(solution)/shard_map/ppermute | solution.py:383
  29.5 2.9 %shard_map.130 = (f32[1024,128]{1,0:T(8,128)S(1)}, f32[1024,128]{1,0:T(8,128)S(1)}) custom-call(s32[5]{0:T(128)S(1)} %stack.19.place_ref, bf16[1024,128]{1,0:T(8,128)(2,1)S(1)} %get-tuple-element.29.qn, f32[1024,128]{1,0:T(8,128)S(1)} %get-tuple-element.30.acc_ref, f32[1024,128]{1,0:T(8,128)S(1)} %get-tuple-element.31.total_ref, ...), custom_call_target="tpu_custom_call" | custom-call | tf_op jit(solution)/shard_map/pallas_call | solution.py:165
  32.5 4.3 %shard_map.131 = bf16[16,16,4096]{2,1,0:T(8,128)(2,1)S(1)} custom-call(s32[5]{0:T(128)S(1)} %stack.19.place_ref, bf16[1024,128]{1,0:T(8,128)(2,1)S(1)} %get-tuple-element.29.qn, f32[1024,128]{1,0:T(8,128)S(1)} %get-tuple-element.35.acc_ref, f32[1024,128]{1,0:T(8,128)S(1)} %get-tuple-element.36.total_ref, bf16[768,256]{1,0:T(8,128)(2,1)S(1)} %collective-permute-done.4.first, ...), custom_call_target="tpu_custom_call" | custom-call | tf_op jit(solution)/shard_map/pallas_call | solution.py:195
  36.8 35.2 %all_to_all.15.parts_ref = bf16[16,16,4096]{2,1,0:T(8,128)(2,1)S(1)} all-to-all(bf16[16,16,4096]{2,1,0:T(8,128)(2,1)S(1)} %shard_map.131), channel_id=1, replica_groups=mesh['z'=4,'y'=4,'x'=4,'c'=2] {'z','y'}, dimensions={0} | all-to-all | bytes 4194304 | tf_op jit(solution)/shard_map/all_to_all | solution.py:391
  72.1 1.1 shard_map.132
  73.2 38.9 %all_to_all.16.lines_ref = bf16[128,16,512]{2,1,0:T(8,128)(2,1)S(1)} all-to-all(bf16[128,16,512]{2,1,0:T(8,128)(2,1)S(1)} %get-tuple-element.38), channel_id=1, replica_groups=mesh['z'=4,'y'=4,'x'=4,'c'=2] {'z','y','x','c'}, dimensions={0} | all-to-all | bytes 4194304 | tf_op jit(solution)/shard_map/all_to_all | solution.py:394
  112.1 6.8 %shard_map.133 = bf16[128,16,512]{2,1,0:T(8,128)(2,1)S(1)} custom-call(bf16[128,16,512]{2,1,0:T(8,128)(2,1)S(1)} %all_to_all.16.lines_ref, bf16[4096,1536]{1,0:T(8,128)(2,1)S(1)} %bitcast.14, bf16[768,4096]{1,0:T(8,128)(2,1)S(1)} %bitcast.17), custom_call_target="tpu_custom_call" | custom-call | tf_op jit(solution)/shard_map/pallas_call | solution.py:326
  119.0 34.4 %all_to_all.17.lines_ref = bf16[128,16,512]{2,1,0:T(8,128)(2,1)S(1)} all-to-all(bf16[128,16,512]{2,1,0:T(8,128)(2,1)S(1)} %shard_map.133), channel_id=1, replica_groups=mesh['z'=4,'y'=4,'x'=4,'c'=2] {'z','y','x','c'}, dimensions={0} | all-to-all | bytes 4194304 | tf_op jit(solution)/shard_map/all_to_all | solution.py:396
  153.4 1.1 shard_map.134
  (35 shorter events, 3.4 us)
Async XLA Ops:
  0.0 20.5 %copy-start = (bf16[256,512]{1,0:T(8,128)(2,1)S(1)}, bf16[256,512]{1,0:T(8,128)(2,1)}, u32[]{:S(2)}) copy-start(bf16[256,512]{1,0:T(8,128)(2,1)} %q_ref) | copy-start | bytes 786436
  0.0 20.5 %copy-start.3 = (f32[128]{0:T(128)S(1)}, f32[128]{0:T(128)}, u32[]{:S(2)}) copy-start(f32[128]{0:T(128)} %param.16) | copy-start | bytes 1540
  0.8 0.7 copy-start.4
  1.4 110.6 %slice-start.3 = ((s8[6291456]{0:T(1024)(128)(4,1)}), s8[2097152]{0:T(1024)(128)(4,1)S(1)}, s32[]{:S(2)}) async-start(s8[6291456]{0:T(1024)(128)(4,1)} %bitcast.15), calls=%async_computation.6 | async-start | bytes 4194304
  3.4 17.1 %collective-permute-start.3 = (bf16[768,256]{1,0:T(8,128)(2,1)S(1)}, bf16[768,256]{1,0:T(8,128)(2,1)S(1)}, u32[]{:S(2)}, u32[]{:S(2)}) collective-permute-start(bf16[768,256]{1,0:T(8,128)(2,1)S(1)} %shard_map.127.own_ref), channel_id=1, source_target_pairs={{0,1},{1,0},{2,3},{3,2},{4,5},{5,4},{6,7},{7,6},{8,9},{9,8},{10,11... | collective-permute-start | bytes 1179656 | tf_op jit(solution)/shard_map/ppermute | solution.py:382
  4.9 19.3 %collective-permute-start.2 = (bf16[768,256]{1,0:T(8,128)(2,1)S(1)}, bf16[768,256]{1,0:T(8,128)(2,1)S(1)}, u32[]{:S(2)}, u32[]{:S(2)}) collective-permute-start(bf16[768,256]{1,0:T(8,128)(2,1)S(1)} %shard_map.127.own_ref), channel_id=1, source_target_pairs={{0,6},{2,0},{4,2},{6,4},{1,7},{3,1},{5,3},{7,5},{8,14},{10,8},{12,... | collective-permute-start | bytes 1179656 | tf_op jit(solution)/shard_map/ppermute | solution.py:383
  7.5 16.8 %collective-permute-start.1 = (bf16[768,256]{1,0:T(8,128)(2,1)S(1)}, bf16[768,256]{1,0:T(8,128)(2,1)}, u32[]{:S(2)}, u32[]{:S(2)}) collective-permute-start(bf16[768,256]{1,0:T(8,128)(2,1)S(1)} %shard_map.127.own_ref), channel_id=1, source_target_pairs={{0,4},{2,6},{4,0},{6,2},{1,5},{3,7},{5,1},{7,3},{8,12},{10,14},{12... | collective-permute-start | bytes 1179656 | tf_op jit(solution)/shard_map/ppermute | solution.py:383
  8.0 20.6 %collective-permute-start = (bf16[768,256]{1,0:T(8,128)(2,1)S(1)}, bf16[768,256]{1,0:T(8,128)(2,1)}, u32[]{:S(2)}, u32[]{:S(2)}) collective-permute-start(bf16[768,256]{1,0:T(8,128)(2,1)S(1)} %shard_map.127.own_ref), channel_id=1, source_target_pairs={{0,2},{2,4},{4,6},{6,0},{1,3},{3,5},{5,7},{7,1},{8,10},{10,12},{12... | collective-permute-start | bytes 1179656 | tf_op jit(solution)/shard_map/ppermute | solution.py:383
  20.5 91.6 %slice-start = ((s8[12582912]{0:T(1024)(128)(4,1)}), s8[4194304]{0:T(1024)(128)(4,1)S(1)}, s32[]{:S(2)}) async-start(s8[12582912]{0:T(1024)(128)(4,1)} %bitcast.12), calls=%async_computation.3 | async-start | bytes 8388608
  28.5 3.9 %collective-permute-start.4 = (bf16[768,256]{1,0:T(8,128)(2,1)}, bf16[768,256]{1,0:T(8,128)(2,1)S(1)}, u32[]{:S(2)}, u32[]{:S(2)}) collective-permute-start(bf16[768,256]{1,0:T(8,128)(2,1)} %collective-permute-done.first), channel_id=1, source_target_pairs={{0,1},{1,0},{2,3},{3,2},{4,5},{5,4},{6,7},{7,6},{8,9},{9,8},{10,11... | collective-permute-start | bytes 1179656 | tf_op jit(solution)/shard_map/ppermute | solution.py:388
  29.0 3.4 %collective-permute-start.5 = (bf16[768,256]{1,0:T(8,128)(2,1)}, bf16[768,256]{1,0:T(8,128)(2,1)S(1)}, u32[]{:S(2)}, u32[]{:S(2)}) collective-permute-start(bf16[768,256]{1,0:T(8,128)(2,1)} %collective-permute-done.1.second), channel_id=1, source_target_pairs={{0,1},{1,0},{2,3},{3,2},{4,5},{5,4},{6,7},{7,6},{8,9},{9,8},{10,11... | collective-permute-start | bytes 1179656 | tf_op jit(solution)/shard_map/ppermute | solution.py:388
  29.1 3.4 %collective-permute-start.6 = (bf16[768,256]{1,0:T(8,128)(2,1)S(1)}, bf16[768,256]{1,0:T(8,128)(2,1)S(1)}, u32[]{:S(2)}, u32[]{:S(2)}) collective-permute-start(bf16[768,256]{1,0:T(8,128)(2,1)S(1)} %collective-permute-done.2.third), channel_id=1, source_target_pairs={{0,1},{1,0},{2,3},{3,2},{4,5},{5,4},{6,7},{7,6},{8,9},{9,8},{10,11... | collective-permute-start | bytes 1179656 | tf_op jit(solution)/shard_map/ppermute | solution.py:388
  32.4 39.6 %copy-start.1 = (bf16[16,4096]{1,0:T(8,128)(2,1)S(1)}, bf16[16,4096]{1,0:T(8,128)(2,1)}, u32[]{:S(2)}) copy-start(bf16[16,4096]{1,0:T(8,128)(2,1)} %residual_ref.1) | copy-start | bytes 393220
  32.5 39.6 %copy-start.2 = (f32[4096]{0:T(1024)S(1)}, f32[4096]{0:T(1024)}, u32[]{:S(2)}) copy-start(f32[4096]{0:T(1024)} %param.20) | copy-start | bytes 49156
  32.5 79.6 %slice-start.1 = ((s8[12582912]{0:T(1024)(128)(4,1)}), s8[4194304]{0:T(1024)(128)(4,1)S(1)}, s32[]{:S(2)}) async-start(s8[12582912]{0:T(1024)(128)(4,1)} %bitcast.12), calls=%async_computation.4 | async-start | bytes 8388608
  32.5 79.6 %slice-start.4 = ((s8[6291456]{0:T(1024)(128)(4,1)}), s8[4194304]{0:T(1024)(128)(4,1)S(1)}, s32[]{:S(2)}) async-start(s8[6291456]{0:T(1024)(128)(4,1)} %bitcast.15), calls=%async_computation.7 | async-start | bytes 8388608
  36.8 75.3 %slice-start.2 = ((s8[12582912]{0:T(1024)(128)(4,1)}), s8[4194304]{0:T(1024)(128)(4,1)S(1)}, s32[]{:S(2)}) async-start(s8[12582912]{0:T(1024)(128)(4,1)} %bitcast.12), calls=%async_computation.5 | async-start | bytes 8388608

commit v3 on v2

--- a/solution.py
+++ b/solution.py
@@ -52,37 +52,62 @@
     return [(i, (i + step) % 4) for i in range(4)]
 
 
-def prep_kernel(place_ref, cache_ref, new_ref, gain_ref, out_ref, cache, new, sems):
-    head = place_ref[1]
+def prep_kernel(
+    place_ref, cache_ref, new_ref, gain_ref, out_ref, part_ref, cache, new, gain, sems
+):
+    head, quarter = place_ref[1], place_ref[2]
     copies = (
-        pltpu.make_async_copy(cache_ref.at[head], cache, sems.at[0]),
+        pltpu.make_async_copy(gain_ref, gain, sems.at[0]),
         pltpu.make_async_copy(new_ref.at[head], new, sems.at[1]),
+        pltpu.make_async_copy(cache_ref.at[head], cache, sems.at[2]),
     )
     for copy in copies:
         copy.start()
+    copies[0].wait()
     for copy, ref, start, rows in (
         (copies[1], new, CACHE_ROWS, QROWS),
-        (copies[0], cache, 0, CACHE_ROWS),
+        (copies[2], cache, 0, CACHE_ROWS),
     ):
         copy.wait()
-        keys = rms_scale(ref[:, :HD].astype(F32), gain_ref[...]).astype(BF16)
+        keys = rms_scale(ref[:, :HD].astype(F32), gain[...]).astype(BF16)
         out_ref[pl.ds(start, rows), :HD] = keys
         out_ref[pl.ds(start, rows), HD:] = ref[:, HD:]
+    for start, there, rows in quarter_rows(quarter):
+        part_ref[pl.ds(there, rows), :] = out_ref[pl.ds(start, rows), :]
+
+
+def quarter_rows(quarter):
+    cache_rows, new_rows = CACHE_ROWS // 4, QROWS // 4
+    return (
+        (pl.multiple_of(quarter * cache_rows, cache_rows), 0, cache_rows),
+        (pl.multiple_of(CACHE_ROWS + quarter * new_rows, new_rows), cache_rows, new_rows),
+    )
 
 
 def prep(place, cache, new_kv, k_gain):
     return pl.pallas_call(
         prep_kernel,
-        in_specs=[SMEM(), HBM(), HBM(), VMEM()],
-        out_specs=VMEM(),
-        out_shape=jax.ShapeDtypeStruct((SHARD, 2 * HD), BF16),
+        in_specs=[SMEM(), HBM(), HBM(), HBM()],
+        out_specs=[VMEM()] * 2,
+        out_shape=[
+            jax.ShapeDtypeStruct((SHARD, 2 * HD), BF16),
+            jax.ShapeDtypeStruct((SHARD // 4, 2 * HD), BF16),
+        ],
         scratch_shapes=[
             pltpu.VMEM((CACHE_ROWS, 2 * HD), BF16),
             pltpu.VMEM((QROWS, 2 * HD), BF16),
-            pltpu.SemaphoreType.DMA((2,)),
+            pltpu.VMEM((1, HD), F32),
+            pltpu.SemaphoreType.DMA((3,)),
         ],
         compiler_params=params(8),
     )(place, cache, new_kv, k_gain)
+
+
+def join(place_ref, parts, whole):
+    y = place_ref[2]
+    for k, part in enumerate(parts):
+        for start, there, rows in quarter_rows(lax.rem(y + 4 - k, 4)):
+            whole[pl.ds(start, rows), :] = part[pl.ds(there, rows), :]
 
 
 def seen_blocks(place_ref, core_offset, distances, shards, qn, acc, total):
@@ -129,10 +154,7 @@
                 block(ref, CACHE_ROWS, QROWS, None)
 
 
-def near_kernel(place_ref, q_ref, gain_ref, own_ref, other_ref, qn, acc, total):
-    for h in range(QHEADS):
-        head = q_ref[:, h * HD : (h + 1) * HD].astype(F32)
-        qn[pl.ds(h * QROWS, QROWS), :] = rms_scale(head, gain_ref[...]).astype(BF16)
+def near_kernel(place_ref, qn, own_ref, other_ref, acc, total):
     acc[...] = jnp.zeros_like(acc)
     total[...] = jnp.zeros_like(total)
     seen_blocks(place_ref, 0, (0,), (own_ref,), qn, acc, total)
@@ -145,41 +167,44 @@
 )
 
 
-def attend_near(place, queries, q_gain, own, other):
+def attend_near(place, qn, own, other):
     return pl.pallas_call(
         near_kernel,
-        in_specs=[SMEM()] + [VMEM()] * 4,
-        out_specs=[VMEM()] * 3,
-        out_shape=[jax.ShapeDtypeStruct((QHEADS * QROWS, HD), BF16), *STATE],
-        compiler_params=params(16),
-    )(place, queries, q_gain, own, other)
-
-
-def far_kernel(place_ref, qn, acc_ref, total_ref, first, second, third, acc, total):
-    acc[...] = acc_ref[...]
-    total[...] = total_ref[...]
-    seen_blocks(place_ref, 0, (1, 2, 3), (first, second, third), qn, acc, total)
-
-
-def attend_far(place, qn, acc, total, shards):
-    return pl.pallas_call(
-        far_kernel,
-        in_specs=[SMEM()] + [VMEM()] * 6,
+        in_specs=[SMEM()] + [VMEM()] * 3,
         out_specs=[VMEM()] * 2,
         out_shape=list(STATE),
         compiler_params=params(16),
+    )(place, qn, own, other)
+
+
+def far_kernel(place_ref, qn, acc_ref, total_ref, *refs):
+    first, third, parts, (acc, total, second) = refs[0], refs[1], refs[2:6], refs[6:]
+    acc[...] = acc_ref[...]
+    total[...] = total_ref[...]
+    join(place_ref, parts, second)
+    seen_blocks(place_ref, 0, (1, 3, 2), (first, third, second), qn, acc, total)
+
+
+def attend_far(place, qn, acc, total, shards):
+    return pl.pallas_call(
+        far_kernel,
+        in_specs=[SMEM()] + [VMEM()] * 9,
+        out_specs=[VMEM()] * 2,
+        out_shape=list(STATE),
+        scratch_shapes=[pltpu.VMEM((SHARD, 2 * HD), BF16)],
+        compiler_params=params(16),
     )(place, qn, acc, total, *shards)
 
 
-def last_kernel(
-    place_ref, qn, acc_ref, total_ref, first, second, third, weight_ref, out_ref, acc, total, attn,
-    weight, sem,
-):
+def last_kernel(place_ref, qn, acc_ref, total_ref, *refs):
+    first, third, parts, refs = refs[0], refs[1], refs[2:6], refs[6:]
+    weight_ref, out_ref, acc, total, attn, weight, second, sem = refs
     copy = pltpu.make_async_copy(weight_ref, weight, sem)
     copy.start()
     acc[...] = acc_ref[...]
     total[...] = total_ref[...]
-    seen_blocks(place_ref, 1, (1, 2, 3), (first, second, third), qn, acc, total)
+    join(place_ref, parts, second)
+    seen_blocks(place_ref, 1, (1, 3, 2), (first, third, second), qn, acc, total)
     for h in range(QHEADS):
         at = pl.ds(h * QROWS, QROWS)
         whole = jnp.sum(total[at, :], axis=1, keepdims=True)
@@ -194,7 +219,7 @@
 def attend_last(place, qn, acc, total, shards, weight):
     return pl.pallas_call(
         last_kernel,
-        in_specs=[SMEM()] + [VMEM()] * 6 + [HBM()],
+        in_specs=[SMEM()] + [VMEM()] * 9 + [HBM()],
         out_specs=VMEM(),
         out_shape=jax.ShapeDtypeStruct((GROUPS, ROWS, WIDTH), BF16),
         scratch_shapes=[
@@ -202,51 +227,75 @@
             pltpu.VMEM((QHEADS * QROWS, HD), F32),
             pltpu.VMEM((QROWS, QHEADS * HD), BF16),
             pltpu.VMEM((QHEADS * HD, WIDTH), BF16),
+            pltpu.VMEM((SHARD, 2 * HD), BF16),
             pltpu.SemaphoreType.DMA,
         ],
         compiler_params=params(20),
     )(place, qn, acc, total, *shards, weight)
 
 
-def route_kernel(columns_ref, rows_ref, mix_ref, placing_ref, mixing_ref):
-    line = lax.broadcasted_iota(jnp.int32, (EXPERTS * LINES, EXPERTS), 0)
-    lane = lax.broadcasted_iota(jnp.int32, (EXPERTS * LINES, EXPERTS), 1)
-    slot = (line // LINES) * SLOTS + line % SLOTS
-    hit = slot == columns_ref[0:1, :]
-    for k in range(1, 8):
-        hit = hit | (slot == columns_ref[k : k + 1, :])
-    hit = hit & ((line // SLOTS) % CHUNKS == lane // ROWS)
-    placing_ref[...] = jnp.where(hit, 1.0, 0.0).astype(BF16)
-    line = lax.broadcasted_iota(jnp.int32, (EXPERTS, EXPERTS * LINES), 1)
-    row = lax.broadcasted_iota(jnp.int32, (EXPERTS, EXPERTS * LINES), 0)
-    slot = (line // LINES) * SLOTS + line % SLOTS
-    value = jnp.zeros(slot.shape, F32)
+def route_kernel(
+    ids_hbm, weights_hbm, q_ref, gain_ref, placing_ref, mixing_ref, qn,
+    ids_ref, weights_ref, queries, gain, sems,
+):
+    pairs = ((gain_ref, gain), (q_ref, queries), (ids_hbm, ids_ref), (weights_hbm, weights_ref))
+    copies = [pltpu.make_async_copy(a, b, sems.at[i]) for i, (a, b) in enumerate(pairs)]
+    for copy in copies:
+        copy.start()
+    for copy in copies:
+        copy.wait()
+    square = (EXPERTS, EXPERTS)
+    expert = lax.broadcasted_iota(jnp.int32, square, 0)
+    lane = lax.broadcasted_iota(jnp.int32, square, 1)
+    row = lax.broadcasted_iota(jnp.int32, (ROWS, EXPERTS), 0)
+    spread = lax.broadcasted_iota(jnp.int32, (ROWS, EXPERTS), 1) % ROWS == row
+    spread = jnp.where(spread, 1.0, 0.0).astype(BF16)
+    ids = jnp.dot(ids_ref[...].astype(F32).astype(BF16), spread, preferred_element_type=F32)
+    ids = ids.astype(jnp.int32)
+    weights = jnp.dot(weights_ref[...], spread, preferred_element_type=F32)
+    named = jnp.zeros(square, F32)
+    value = jnp.zeros(square, F32)
     for k in range(8):
-        value = jnp.where(slot == rows_ref[:, k : k + 1], mix_ref[:, k : k + 1], value)
-    same = (line // SLOTS) % CHUNKS == row // ROWS
-    mixing_ref[...] = jnp.where(same, value, 0.0).astype(BF16)
-
-
-def route(expert_ids, combine_weight):
-    flat = expert_ids.reshape(-1)
-    index = jnp.arange(flat.shape[0], dtype=jnp.int32)
-    earlier = (flat[:, None] == flat[None, :]) & (index[None, :] < index[:, None])
-    slot = jnp.sum(earlier.astype(jnp.int32), axis=1)
-    target = (flat * SLOTS + slot).reshape(expert_ids.shape)
+        hit = expert == ids[k : k + 1, :]
+        named = jnp.where(hit, 1.0, named)
+        value = jnp.where(hit, weights[k : k + 1, :], value)
+    earlier = (expert // ROWS == lane // ROWS) & (expert < lane)
+    before = jnp.dot(
+        named.astype(BF16), jnp.where(earlier, 1.0, 0.0).astype(BF16), preferred_element_type=F32
+    )
+    lines = (EXPERTS * LINES, EXPERTS)
+    line = lax.broadcasted_iota(jnp.int32, lines, 0)
+    column = lax.broadcasted_iota(jnp.int32, lines, 1)
+    same = (line // SLOTS) % CHUNKS == column // ROWS
+    of_expert = line // LINES == column
+    for out_ref, held in ((placing_ref, named), (mixing_ref, value)):
+        table = jnp.zeros(lines, F32)
+        for s in range(SLOTS):
+            pick = jnp.where(of_expert & (line % SLOTS == s), 1.0, 0.0).astype(BF16)
+            slot = jnp.where(before == s, held, 0.0).astype(BF16)
+            table = table + jnp.dot(pick, slot, preferred_element_type=F32)
+        out_ref[...] = jnp.where(same, table, 0.0).astype(BF16)
+    for h in range(QHEADS):
+        head = queries[:, h * HD : (h + 1) * HD].astype(F32)
+        qn[pl.ds(h * QROWS, QROWS), :] = rms_scale(head, gain[...]).astype(BF16)
+
+
+def route(expert_ids, combine_weight, queries, q_gain):
     return pl.pallas_call(
         route_kernel,
-        in_specs=[VMEM()] * 3,
-        out_specs=[VMEM()] * 2,
-        out_shape=[
-            jax.ShapeDtypeStruct((EXPERTS * LINES, EXPERTS), BF16),
-            jax.ShapeDtypeStruct((EXPERTS, EXPERTS * LINES), BF16),
-        ],
-        compiler_params=params(12),
-    )(
-        jnp.tile(target.T, (1, CHUNKS)),
-        jnp.tile(target, (CHUNKS, 1)),
-        jnp.tile(combine_weight.astype(F32), (CHUNKS, 1)),
-    )
+        in_specs=[HBM()] * 4,
+        out_specs=[VMEM()] * 3,
+        out_shape=[jax.ShapeDtypeStruct((EXPERTS * LINES, EXPERTS), BF16)] * 2
+        + [jax.ShapeDtypeStruct((QHEADS * QROWS, HD), BF16)],
+        scratch_shapes=[
+            pltpu.VMEM((8, ROWS), jnp.int32),
+            pltpu.VMEM((8, ROWS), BF16),
+            pltpu.VMEM((QROWS, QHEADS * HD), BF16),
+            pltpu.VMEM((1, HD), F32),
+            pltpu.SemaphoreType.DMA((4,)),
+        ],
+        compiler_params=params(16),
+    )(expert_ids, combine_weight, queries, q_gain)
 
 
 def dispatch_kernel(parts_ref, residual_ref, gain_ref, placing_ref, hidden_ref, out_ref, pieces):
@@ -342,7 +391,9 @@
 
 def combine_kernel(lines_ref, mixing_ref, hidden_ref, out_ref):
     lines = lines_ref[...].reshape(EXPERTS * LINES, PIECE)
-    mixed = jnp.dot(mixing_ref[...], lines, preferred_element_type=F32)
+    mixed = lax.dot_general(
+        mixing_ref[...], lines, (((0,), (0,)), ((), ())), preferred_element_type=F32
+    )
     for k in range(CHUNKS):
         columns = slice(k * PIECE, (k + 1) * PIECE)
         value = hidden_ref[:, columns] + mixed[k * ROWS : (k + 1) * ROWS, :]
@@ -377,15 +428,23 @@
     z, y, x, c = (lax.axis_index(name).astype(jnp.int32) for name in ("z", "y", "x", "c"))
     place = jnp.stack([prefix_len[0], z, y, x, c])
     held = functools.partial(pltpu.with_memory_space_constraint, memory_space=pltpu.HBM)
-    own = prep(place, held(cache), held(new_kv), k_gain.reshape(1, HD))
+    own, part = prep(place, held(cache), held(new_kv), held(k_gain.reshape(1, HD)))
     swap = functools.partial(lax.ppermute, axis_name="c", perm=[(0, 1), (1, 0)])
     other = swap(own)
-    near = [lax.ppermute(own, "x", shift(k)) for k in (1, 2, 3)]
-    placing, mixing = route(expert_ids, combine_weight)
-    queries, placing, mixing = lax.optimization_barrier((queries, placing, mixing))
-    qn, acc, total = attend_near(place, queries, q_gain.reshape(1, HD), own, other)
+    parts = [lax.ppermute(part, "x", shift(2))]
+    placing, mixing, qn = route(
+        held(expert_ids.T), held(combine_weight.T), held(queries), held(q_gain.reshape(1, HD))
+    )
+    whole, parts[0], placing, mixing, qn = lax.optimization_barrier(
+        (own, parts[0], placing, mixing, qn)
+    )
+    part = swap(parts[0])
+    near = [lax.ppermute(whole, "x", shift(k)) for k in (1, 3)]
+    parts += [lax.ppermute(parts[0], "y", shift(k)) for k in (1, 2, 3)]
+    acc, total = attend_near(place, qn, own, other)
+    near = near + parts
     *near, qn, acc, total = lax.optimization_barrier((*near, qn, acc, total))
-    far = [swap(shard) for shard in near]
+    far = [swap(near[0]), swap(near[1]), part] + [swap(shard) for shard in near[3:]]
     acc, total = attend_far(place, qn, acc, total, near)
     parts = attend_last(place, qn, acc, total, far, held(out_weight))
     parts = lax.all_to_all(parts, ("z", "y"), split_axis=0, concat_axis=0, tiled=True)

time: 155 us -> 151 us (0.974)
  local copies, waits for them, and re-layouts: 8.58 us -> 0.13 us
  starting transfers between devices: 6.21 us -> 14.4 us
    ppermute x6 -> x12, starting transfers between devices: 4.7 us -> 13.4 us  [the longest x3 3.78 us: per_device(): parts += [lax.ppermute(parts[0], 'y', shift(k)) for k in (1, 2, 3)]]
    another operation x4 -> x0, local copies, waits for them, and re-layouts: 2.85 us -> none  [the longest x2 1.45 us: route(): jnp.tile(target.T, (1, CHUNKS))]
    unnamed x21 -> x14, local copies, waits for them, and re-layouts: 2.06 us -> 0.04 us
    ppermute x6 -> x12, waiting for transfers between devices: 4.66 us -> 3.83 us  [the longest x3 2.13 us: per_device(): parts += [lax.ppermute(parts[0], 'y', shift(k)) for k in (1, 2, 3)]]
  transfers between devices with their start and end apart: 7 -> 13, of which waited for: 2 -> 4; matrix products, arithmetic and copies ran while one was open for 6% -> 0% of each run, Pallas kernels for 6% -> 6%
where the time goes in v3:
time: 151 us
  blocking collectives  108 us (72%)
  Pallas kernels  23.8 us (16%)
  starting transfers between devices  14.4 us (10%)
  waiting for transfers between devices  3.83 us (3%)
    all_to_all x2, blocking collectives, per_device(): lax.all_to_all(lines, everyone, split_axis=0, concat_axis=0, tiled=True)  71.9 us
    all_to_all x1, blocking collectives, per_device(): lax.all_to_all(parts, ('z', 'y'), split_axis=0, concat_axis=0, tiled=True)  35.7 us
    pallas_call x1, Pallas kernels, experts(): pl.pallas_call(expert_kernel, in_specs=[VMEM(), VMEM(), HBM()], out_specs...  6.83 us
    pallas_call x1, Pallas kernels, attend_last(): pl.pallas_call(last_kernel, in_specs=[SMEM()] + [VMEM()] * 9 + [HBM()], o...  4.32 us
    ppermute x3, starting transfers between devices, per_device(): parts += [lax.ppermute(parts[0], 'y', shift(k)) for k in (1, 2, 3)]  3.78 us
    ppermute x1, starting transfers between devices, per_device(): parts = [lax.ppermute(part, 'x', shift(2))]  3.65 us
    pallas_call x1, Pallas kernels, attend_near(): pl.pallas_call(near_kernel, in_specs=[SMEM()] + [VMEM()] * 3, out_specs=[...  3.14 us
    pallas_call x1, Pallas kernels, attend_far(): pl.pallas_call(far_kernel, in_specs=[SMEM()] + [VMEM()] * 9, out_specs=[V...  3.06 us
  transfers between devices with their start and end apart: 13, of which 4 were waited for; matrix products, arithmetic and copies ran while one was open for 0% of the time, Pallas kernels for 6%

profile of v3, /device:TPU:1, one launch (start us, length us, event | category | flops | bytes accessed | tf_op | source)
XLA Modules:
  0.0 150.6 jit_solution(14965109844532772004)
XLA Ops:
  0.7 2.1 %shard_map.127 = (bf16[768,256]{1,0:T(8,128)(2,1)S(1)}, bf16[192,256]{1,0:T(8,128)(2,1)S(1)}) custom-call(s32[5]{0:T(128)S(1)} %stack.19.place_ref, bf16[4,512,256]{2,1,0:T(8,128)(2,1)} %cache_ref.1, bf16[4,256,256]{2,1,0:T(8,128)(2,1)} %new_ref.1, f32[1,128]{1,0:T(1,128)} %bitcast.20), custom_call_target="tpu_custom_call" | custom-call | tf_op jit(solution)/shard_map/pallas_call | solution.py:88
  2.8 3.7 %collective-permute-start = (bf16[192,256]{1,0:T(8,128)(2,1)S(1)}, bf16[192,256]{1,0:T(8,128)(2,1)S(1)}, u32[]{:S(2)}, u32[]{:S(2)}) collective-permute-start(bf16[192,256]{1,0:T(8,128)(2,1)S(1)} %get-tuple-element.31), channel_id=1, source_target_pairs={{0,4},{2,6},{4,0},{6,2},{1,5},{3,7},{5,1},{7,3},{8,12},{10,14},{12... | collective-permute-start | bytes 294920 | tf_op jit(solution)/shard_map/ppermute | solution.py:434
  6.5 1.0 collective-permute-start.6
  7.4 2.2 %shard_map.128 = (bf16[2048,128]{1,0:T(8,128)(2,1)S(1)}, bf16[2048,128]{1,0:T(8,128)(2,1)S(1)}, bf16[1024,128]{1,0:T(8,128)(2,1)S(1)}) custom-call(s32[8,16]{1,0:T(8,128)} %bitcast.18, bf16[8,16]{1,0:T(8,128)(2,1)} %bitcast.19, bf16[256,512]{1,0:T(8,128)(2,1)} %q_ref.1, f32[1,128]{1,0:T(1,128)} %bitcast.21), custom_call_target="tpu_custom_call" | custom-call | tf_op jit(solution)/shard_map/pallas_call | solution.py:284
  9.6 1.6 %collective-permute-start.2 = (bf16[768,256]{1,0:T(8,128)(2,1)S(1)}, bf16[768,256]{1,0:T(8,128)(2,1)S(1)}, u32[]{:S(2)}, u32[]{:S(2)}) collective-permute-start(bf16[768,256]{1,0:T(8,128)(2,1)S(1)} %get-tuple-element.35.own_ref), channel_id=1, source_target_pairs={{0,6},{2,0},{4,2},{6,4},{1,7},{3,1},{5,3},{7,5},{8,14},{10,8},{12,... | collective-permute-start | bytes 1179656 | tf_op jit(solution)/shard_map/ppermute | solution.py:442
  11.2 2.7 %collective-permute-start.5 = (bf16[192,256]{1,0:T(8,128)(2,1)S(1)}, bf16[192,256]{1,0:T(8,128)(2,1)S(1)}, u32[]{:S(2)}, u32[]{:S(2)}) collective-permute-start(bf16[192,256]{1,0:T(8,128)(2,1)S(1)} %collective-permute-done.refs_2_), channel_id=1, source_target_pairs={{0,24},{8,0},{16,8},{24,16},{1,25},{9,1},{17,9},{25,17},{2,26},{10... | collective-permute-start | bytes 294920 | tf_op jit(solution)/shard_map/ppermute | solution.py:443
  14.3 0.7 collective-permute-start.3
  15.0 3.1 %shard_map.129 = (f32[1024,128]{1,0:T(8,128)S(1)}, f32[1024,128]{1,0:T(8,128)S(1)}) custom-call(s32[5]{0:T(128)S(1)} %stack.19.place_ref, bf16[1024,128]{1,0:T(8,128)(2,1)S(1)} %get-tuple-element.40.qn, bf16[768,256]{1,0:T(8,128)(2,1)S(1)} %get-tuple-element.35.own_ref, bf16[768,256]{1,0:T(8,128)(2,1)S(1)} %collective-permute-done.6.other_ref), custom_call_target="tpu_custom_call" | custom-call | tf_op jit(solution)/shard_map/pallas_call | solution.py:171
  18.1 0.9 collective-permute-done.4.refs_4_
  19.0 1.2 collective-permute-done.3.refs_3_
  20.2 0.7 collective-permute-done.1.refs_0_
  20.9 3.0 %collective-permute-start.7 = (bf16[768,256]{1,0:T(8,128)(2,1)S(1)}, bf16[768,256]{1,0:T(8,128)(2,1)S(1)}, u32[]{:S(2)}, u32[]{:S(2)}) collective-permute-start(bf16[768,256]{1,0:T(8,128)(2,1)S(1)} %collective-permute-done.1.refs_0_), channel_id=1, source_target_pairs={{0,1},{1,0},{2,3},{3,2},{4,5},{5,4},{6,7},{7,6},{8,9},{9,8},{10,11... | collective-permute-start | bytes 1179656 | tf_op jit(solution)/shard_map/ppermute | solution.py:447
  23.9 0.5 collective-permute-start.9
  24.4 0.5 collective-permute-start.11
  24.9 1.0 collective-permute-done.9.refs_2_
  26.0 0.4 collective-permute-start.12
  26.3 3.1 %shard_map.130 = (f32[1024,128]{1,0:T(8,128)S(1)}, f32[1024,128]{1,0:T(8,128)S(1)}) custom-call(s32[5]{0:T(128)S(1)} %stack.19.place_ref, bf16[1024,128]{1,0:T(8,128)(2,1)S(1)} %get-tuple-element.40.qn, f32[1024,128]{1,0:T(8,128)S(1)} %get-tuple-element.41.acc_ref, f32[1024,128]{1,0:T(8,128)S(1)} %get-tuple-element.42.total_ref, ...), custom_call_target="tpu_custom_call" | custom-call | tf_op jit(solution)/shard_map/pallas_call | solution.py:189
  29.5 4.3 %shard_map.131 = bf16[16,16,4096]{2,1,0:T(8,128)(2,1)S(1)} custom-call(s32[5]{0:T(128)S(1)} %stack.19.place_ref, bf16[1024,128]{1,0:T(8,128)(2,1)S(1)} %get-tuple-element.40.qn, f32[1024,128]{1,0:T(8,128)S(1)} %get-tuple-element.49.acc_ref, f32[1024,128]{1,0:T(8,128)S(1)} %get-tuple-element.50.total_ref, ...), custom_call_target="tpu_custom_call" | custom-call | tf_op jit(solution)/shard_map/pallas_call | solution.py:220
  33.9 35.7 %all_to_all.15.parts_ref = bf16[16,16,4096]{2,1,0:T(8,128)(2,1)S(1)} all-to-all(bf16[16,16,4096]{2,1,0:T(8,128)(2,1)S(1)} %shard_map.131), channel_id=1, replica_groups=mesh['z'=4,'y'=4,'x'=4,'c'=2] {'z','y'}, dimensions={0} | all-to-all | bytes 4194304 | tf_op jit(solution)/shard_map/all_to_all | solution.py:450
  69.6 1.1 shard_map.132
  70.7 37.5 %all_to_all.16.lines_ref = bf16[128,16,512]{2,1,0:T(8,128)(2,1)S(1)} all-to-all(bf16[128,16,512]{2,1,0:T(8,128)(2,1)S(1)} %get-tuple-element.52), channel_id=1, replica_groups=mesh['z'=4,'y'=4,'x'=4,'c'=2] {'z','y','x','c'}, dimensions={0} | all-to-all | bytes 4194304 | tf_op jit(solution)/shard_map/all_to_all | solution.py:453
  108.3 6.8 %shard_map.133 = bf16[128,16,512]{2,1,0:T(8,128)(2,1)S(1)} custom-call(bf16[128,16,512]{2,1,0:T(8,128)(2,1)S(1)} %all_to_all.16.lines_ref, bf16[4096,1536]{1,0:T(8,128)(2,1)S(1)} %bitcast.13, bf16[768,4096]{1,0:T(8,128)(2,1)S(1)} %bitcast.16), custom_call_target="tpu_custom_call" | custom-call | tf_op jit(solution)/shard_map/pallas_call | solution.py:375
  115.1 34.4 %all_to_all.17.lines_ref = bf16[128,16,512]{2,1,0:T(8,128)(2,1)S(1)} all-to-all(bf16[128,16,512]{2,1,0:T(8,128)(2,1)S(1)} %shard_map.133), channel_id=1, replica_groups=mesh['z'=4,'y'=4,'x'=4,'c'=2] {'z','y','x','c'}, dimensions={0} | all-to-all | bytes 4194304 | tf_op jit(solution)/shard_map/all_to_all | solution.py:455
  149.5 1.1 shard_map.134
  (30 shorter events, 0.5 us)
Async XLA Ops:
  0.7 107.5 %slice-start.3 = ((s8[6291456]{0:T(1024)(128)(4,1)}), s8[4194304]{0:T(1024)(128)(4,1)S(1)}, s32[]{:S(2)}) async-start(s8[6291456]{0:T(1024)(128)(4,1)} %bitcast.14), calls=%async_computation.6 | async-start | bytes 8388608
  2.8 6.8 %collective-permute-start = (bf16[192,256]{1,0:T(8,128)(2,1)S(1)}, bf16[192,256]{1,0:T(8,128)(2,1)S(1)}, u32[]{:S(2)}, u32[]{:S(2)}) collective-permute-start(bf16[192,256]{1,0:T(8,128)(2,1)S(1)} %get-tuple-element.31), channel_id=1, source_target_pairs={{0,4},{2,6},{4,0},{6,2},{1,5},{3,7},{5,1},{7,3},{8,12},{10,14},{12... | collective-permute-start | bytes 294920 | tf_op jit(solution)/shard_map/ppermute | solution.py:434
  6.5 7.8 %collective-permute-start.6 = (bf16[768,256]{1,0:T(8,128)(2,1)S(1)}, bf16[768,256]{1,0:T(8,128)(2,1)S(1)}, u32[]{:S(2)}, u32[]{:S(2)}) collective-permute-start(bf16[768,256]{1,0:T(8,128)(2,1)S(1)} %get-tuple-element.35.own_ref), channel_id=1, source_target_pairs={{0,1},{1,0},{2,3},{3,2},{4,5},{5,4},{6,7},{7,6},{8,9},{9,8},{10,11... | collective-permute-start | bytes 1179656 | tf_op jit(solution)/shard_map/ppermute | solution.py:433
  9.6 10.6 %collective-permute-start.2 = (bf16[768,256]{1,0:T(8,128)(2,1)S(1)}, bf16[768,256]{1,0:T(8,128)(2,1)S(1)}, u32[]{:S(2)}, u32[]{:S(2)}) collective-permute-start(bf16[768,256]{1,0:T(8,128)(2,1)S(1)} %get-tuple-element.35.own_ref), channel_id=1, source_target_pairs={{0,6},{2,0},{4,2},{6,4},{1,7},{3,1},{5,3},{7,5},{8,14},{10,8},{12,... | collective-permute-start | bytes 1179656 | tf_op jit(solution)/shard_map/ppermute | solution.py:442
  11.2 9.7 %collective-permute-start.1 = (bf16[768,256]{1,0:T(8,128)(2,1)S(1)}, bf16[768,256]{1,0:T(8,128)(2,1)S(1)}, u32[]{:S(2)}, u32[]{:S(2)}) collective-permute-start(bf16[768,256]{1,0:T(8,128)(2,1)S(1)} %get-tuple-element.35.own_ref), channel_id=1, source_target_pairs={{0,2},{2,4},{4,6},{6,0},{1,3},{3,5},{5,7},{7,1},{8,10},{10,12},{12... | collective-permute-start | bytes 1179656 | tf_op jit(solution)/shard_map/ppermute | solution.py:442
  11.2 6.9 %collective-permute-start.5 = (bf16[192,256]{1,0:T(8,128)(2,1)S(1)}, bf16[192,256]{1,0:T(8,128)(2,1)S(1)}, u32[]{:S(2)}, u32[]{:S(2)}) collective-permute-start(bf16[192,256]{1,0:T(8,128)(2,1)S(1)} %collective-permute-done.refs_2_), channel_id=1, source_target_pairs={{0,24},{8,0},{16,8},{24,16},{1,25},{9,1},{17,9},{25,17},{2,26},{10... | collective-permute-start | bytes 294920 | tf_op jit(solution)/shard_map/ppermute | solution.py:443
  13.9 5.1 %collective-permute-start.4 = (bf16[192,256]{1,0:T(8,128)(2,1)S(1)}, bf16[192,256]{1,0:T(8,128)(2,1)S(1)}, u32[]{:S(2)}, u32[]{:S(2)}) collective-permute-start(bf16[192,256]{1,0:T(8,128)(2,1)S(1)} %collective-permute-done.refs_2_), channel_id=1, source_target_pairs={{0,16},{8,24},{16,0},{24,8},{1,17},{9,25},{17,1},{25,9},{2,18},{10... | collective-permute-start | bytes 294920 | tf_op jit(solution)/shard_map/ppermute | solution.py:443
  14.3 6.0 %collective-permute-start.3 = (bf16[192,256]{1,0:T(8,128)(2,1)S(1)}, bf16[192,256]{1,0:T(8,128)(2,1)S(1)}, u32[]{:S(2)}, u32[]{:S(2)}) collective-permute-start(bf16[192,256]{1,0:T(8,128)(2,1)S(1)} %collective-permute-done.refs_2_), channel_id=1, source_target_pairs={{0,8},{8,16},{16,24},{24,0},{1,9},{9,17},{17,25},{25,1},{2,10},{10... | collective-permute-start | bytes 294920 | tf_op jit(solution)/shard_map/ppermute | solution.py:443
  15.0 93.3 %slice-start = ((s8[12582912]{0:T(1024)(128)(4,1)}), s8[4194304]{0:T(1024)(128)(4,1)S(1)}, s32[]{:S(2)}) async-start(s8[12582912]{0:T(1024)(128)(4,1)} %bitcast.11), calls=%async_computation.3 | async-start | bytes 8388608
  20.9 8.6 %collective-permute-start.7 = (bf16[768,256]{1,0:T(8,128)(2,1)S(1)}, bf16[768,256]{1,0:T(8,128)(2,1)S(1)}, u32[]{:S(2)}, u32[]{:S(2)}) collective-permute-start(bf16[768,256]{1,0:T(8,128)(2,1)S(1)} %collective-permute-done.1.refs_0_), channel_id=1, source_target_pairs={{0,1},{1,0},{2,3},{3,2},{4,5},{5,4},{6,7},{7,6},{8,9},{9,8},{10,11... | collective-permute-start | bytes 1179656 | tf_op jit(solution)/shard_map/ppermute | solution.py:447
  23.9 5.5 %collective-permute-start.8 = (bf16[768,256]{1,0:T(8,128)(2,1)S(1)}, bf16[768,256]{1,0:T(8,128)(2,1)S(1)}, u32[]{:S(2)}, u32[]{:S(2)}) collective-permute-start(bf16[768,256]{1,0:T(8,128)(2,1)S(1)} %collective-permute-done.2.refs_1_), channel_id=1, source_target_pairs={{0,1},{1,0},{2,3},{3,2},{4,5},{5,4},{6,7},{7,6},{8,9},{9,8},{10,11... | collective-permute-start | bytes 1179656 | tf_op jit(solution)/shard_map/ppermute | solution.py:447
  23.9 2.0 %collective-permute-start.9 = (bf16[192,256]{1,0:T(8,128)(2,1)S(1)}, bf16[192,256]{1,0:T(8,128)(2,1)S(1)}, u32[]{:S(2)}, u32[]{:S(2)}) collective-permute-start(bf16[192,256]{1,0:T(8,128)(2,1)S(1)} %collective-permute-done.refs_2_), channel_id=1, source_target_pairs={{0,1},{1,0},{2,3},{3,2},{4,5},{5,4},{6,7},{7,6},{8,9},{9,8},{10,11... | collective-permute-start | bytes 294920 | tf_op jit(solution)/shard_map/ppermute | solution.py:441
  24.4 5.0 %collective-permute-start.10 = (bf16[192,256]{1,0:T(8,128)(2,1)S(1)}, bf16[192,256]{1,0:T(8,128)(2,1)S(1)}, u32[]{:S(2)}, u32[]{:S(2)}) collective-permute-start(bf16[192,256]{1,0:T(8,128)(2,1)S(1)} %collective-permute-done.3.refs_3_), channel_id=1, source_target_pairs={{0,1},{1,0},{2,3},{3,2},{4,5},{5,4},{6,7},{7,6},{8,9},{9,8},{10,11... | collective-permute-start | bytes 294920 | tf_op jit(solution)/shard_map/ppermute | solution.py:447
  24.4 5.0 %collective-permute-start.11 = (bf16[192,256]{1,0:T(8,128)(2,1)S(1)}, bf16[192,256]{1,0:T(8,128)(2,1)S(1)}, u32[]{:S(2)}, u32[]{:S(2)}) collective-permute-start(bf16[192,256]{1,0:T(8,128)(2,1)S(1)} %collective-permute-done.4.refs_4_), channel_id=1, source_target_pairs={{0,1},{1,0},{2,3},{3,2},{4,5},{5,4},{6,7},{7,6},{8,9},{9,8},{10,11... | collective-permute-start | bytes 294920 | tf_op jit(solution)/shard_map/ppermute | solution.py:447
  26.0 3.5 %collective-permute-start.12 = (bf16[192,256]{1,0:T(8,128)(2,1)S(1)}, bf16[192,256]{1,0:T(8,128)(2,1)S(1)}, u32[]{:S(2)}, u32[]{:S(2)}) collective-permute-start(bf16[192,256]{1,0:T(8,128)(2,1)S(1)} %collective-permute-done.5.refs_5_), channel_id=1, source_target_pairs={{0,1},{1,0},{2,3},{3,2},{4,5},{5,4},{6,7},{7,6},{8,9},{9,8},{10,11... | collective-permute-start | bytes 294920 | tf_op jit(solution)/shard_map/ppermute | solution.py:447
  29.5 40.1 %copy-start = (bf16[16,4096]{1,0:T(8,128)(2,1)S(1)}, bf16[16,4096]{1,0:T(8,128)(2,1)}, u32[]{:S(2)}) copy-start(bf16[16,4096]{1,0:T(8,128)(2,1)} %residual_ref.1) | copy-start | bytes 393220
  29.5 40.1 %copy-start.1 = (f32[4096]{0:T(1024)S(1)}, f32[4096]{0:T(1024)}, u32[]{:S(2)}) copy-start(f32[4096]{0:T(1024)} %param.20) | copy-start | bytes 49156
  29.5 78.7 %slice-start.1 = ((s8[12582912]{0:T(1024)(128)(4,1)}), s8[4194304]{0:T(1024)(128)(4,1)S(1)}, s32[]{:S(2)}) async-start(s8[12582912]{0:T(1024)(128)(4,1)} %bitcast.11), calls=%async_computation.4 | async-start | bytes 8388608
  29.5 78.7 %slice-start.4 = ((s8[6291456]{0:T(1024)(128)(4,1)}), s8[2097152]{0:T(1024)(128)(4,1)S(1)}, s32[]{:S(2)}) async-start(s8[6291456]{0:T(1024)(128)(4,1)} %bitcast.14), calls=%async_computation.7 | async-start | bytes 4194304
  33.8 74.4 %slice-start.2 = ((s8[12582912]{0:T(1024)(128)(4,1)}), s8[4194304]{0:T(1024)(128)(4,1)S(1)}, s32[]{:S(2)}) async-start(s8[12582912]{0:T(1024)(128)(4,1)} %bitcast.11), calls=%async_computation.5 | async-start | bytes 8388608

commit v4 on v3

--- a/solution.py
+++ b/solution.py
@@ -18,6 +18,7 @@
 QHEADS = 4
 CACHE_ROWS = 512
 SHARD = CACHE_ROWS + QROWS
+PART = SHARD // 2
 GROUPS = 16
 EXPERTS = 128
 SLOTS = 2
@@ -52,36 +53,27 @@
     return [(i, (i + step) % 4) for i in range(4)]
 
 
-def prep_kernel(
-    place_ref, cache_ref, new_ref, gain_ref, out_ref, part_ref, cache, new, gain, sems
-):
-    head, quarter = place_ref[1], place_ref[2]
+def prep_kernel(place_ref, cache_ref, new_ref, gain_ref, first, second, cache, new, gain, sems):
+    head = place_ref[1]
     copies = (
         pltpu.make_async_copy(gain_ref, gain, sems.at[0]),
-        pltpu.make_async_copy(new_ref.at[head], new, sems.at[1]),
-        pltpu.make_async_copy(cache_ref.at[head], cache, sems.at[2]),
+        pltpu.make_async_copy(cache_ref.at[head], cache, sems.at[1]),
+        pltpu.make_async_copy(new_ref.at[head], new, sems.at[2]),
     )
     for copy in copies:
         copy.start()
-    copies[0].wait()
-    for copy, ref, start, rows in (
-        (copies[1], new, CACHE_ROWS, QROWS),
-        (copies[2], cache, 0, CACHE_ROWS),
+    for copy in copies:
+        copy.wait()
+    rest = CACHE_ROWS - PART
+    for ref, start, out_ref, there, rows in (
+        (cache, 0, first, 0, PART),
+        (cache, PART, second, 0, rest),
+        (new, 0, second, rest, QROWS),
     ):
-        copy.wait()
-        keys = rms_scale(ref[:, :HD].astype(F32), gain[...]).astype(BF16)
-        out_ref[pl.ds(start, rows), :HD] = keys
-        out_ref[pl.ds(start, rows), HD:] = ref[:, HD:]
-    for start, there, rows in quarter_rows(quarter):
-        part_ref[pl.ds(there, rows), :] = out_ref[pl.ds(start, rows), :]
-
-
-def quarter_rows(quarter):
-    cache_rows, new_rows = CACHE_ROWS // 4, QROWS // 4
-    return (
-        (pl.multiple_of(quarter * cache_rows, cache_rows), 0, cache_rows),
-        (pl.multiple_of(CACHE_ROWS + quarter * new_rows, new_rows), cache_rows, new_rows),
-    )
+        held = ref[pl.ds(start, rows), :]
+        keys = rms_scale(held[:, :HD].astype(F32), gain[...]).astype(BF16)
+        out_ref[pl.ds(there, rows), :HD] = keys
+        out_ref[pl.ds(there, rows), HD:] = held[:, HD:]
 
 
 def prep(place, cache, new_kv, k_gain):
@@ -89,10 +81,7 @@
         prep_kernel,
         in_specs=[SMEM(), HBM(), HBM(), HBM()],
         out_specs=[VMEM()] * 2,
-        out_shape=[
-            jax.ShapeDtypeStruct((SHARD, 2 * HD), BF16),
-            jax.ShapeDtypeStruct((SHARD // 4, 2 * HD), BF16),
-        ],
+        out_shape=[jax.ShapeDtypeStruct((PART, 2 * HD), BF16)] * 2,
         scratch_shapes=[
             pltpu.VMEM((CACHE_ROWS, 2 * HD), BF16),
             pltpu.VMEM((QROWS, 2 * HD), BF16),
@@ -103,19 +92,13 @@
     )(place, cache, new_kv, k_gain)
 
 
-def join(place_ref, parts, whole):
-    y = place_ref[2]
-    for k, part in enumerate(parts):
-        for start, there, rows in quarter_rows(lax.rem(y + 4 - k, 4)):
-            whole[pl.ds(start, rows), :] = part[pl.ds(there, rows), :]
-
-
-def seen_blocks(place_ref, core_offset, distances, shards, qn, acc, total):
-    limit, x, c = place_ref[0], place_ref[3], place_ref[4]
-    core = lax.rem(c + core_offset, 2)
-    tok = x * 2 + c
-
-    def block(ref, start, rows, mask):
+def join(first, second, whole):
+    whole[pl.ds(0, PART), :] = first[...]
+    whole[pl.ds(PART, PART), :] = second[...]
+
+
+def seen_blocks(limit, x, c, own, distances, shards, qn, acc, total):
+    def block(ref, start, rows, mask=None):
         keys = ref[pl.ds(start, rows), :HD]
         values = ref[pl.ds(start, rows), HD:]
         scores = lax.dot_general(
@@ -130,112 +113,137 @@
         total[...] += part
         acc[...] += jnp.dot(weights.astype(BF16), values, preferred_element_type=F32)
 
+    tok = x * 2 + (c if own else 1 - c)
     for distance, ref in zip(distances, shards):
-        owner = lax.rem(x + 4 - distance, 4) * 2 + core
+        owner = lax.rem(x + 4 - distance, 4) * 2 + c
         visible = limit - owner * CACHE_ROWS
-
-        @pl.when(visible >= CACHE_ROWS)
+        whole, earlier = visible >= CACHE_ROWS, owner < tok
+
+        @pl.when(whole & earlier)
         def _():
-            block(ref, 0, CACHE_ROWS, None)
+            block(ref, 0, SHARD)
+
+        @pl.when(whole & jnp.logical_not(earlier))
+        def _():
+            block(ref, 0, CACHE_ROWS)
 
         @pl.when((visible > 0) & (visible < CACHE_ROWS))
         def _():
             key = lax.broadcasted_iota(jnp.int32, (QHEADS * QROWS, CACHE_ROWS), 1)
             block(ref, 0, CACHE_ROWS, key < visible)
 
-        if distance == 0 and core_offset == 0:
+        @pl.when(jnp.logical_not(whole) & earlier)
+        def _():
+            block(ref, CACHE_ROWS, QROWS)
+
+        if own and distance == 0:
             key = lax.broadcasted_iota(jnp.int32, (QHEADS * QROWS, QROWS), 1)
             query = lax.broadcasted_iota(jnp.int32, (QHEADS * QROWS, QROWS), 0)
             block(ref, CACHE_ROWS, QROWS, key <= lax.rem(query, QROWS))
-        else:
-
-            @pl.when(owner < tok)
-            def _():
-                block(ref, CACHE_ROWS, QROWS, None)
-
-
-def near_kernel(place_ref, qn, own_ref, other_ref, acc, total):
-    acc[...] = jnp.zeros_like(acc)
-    total[...] = jnp.zeros_like(total)
-    seen_blocks(place_ref, 0, (0,), (own_ref,), qn, acc, total)
-    seen_blocks(place_ref, 1, (0,), (other_ref,), qn, acc, total)
-
-
-STATE = (
-    jax.ShapeDtypeStruct((QHEADS * QROWS, HD), F32),
-    jax.ShapeDtypeStruct((QHEADS * QROWS, HD), F32),
-)
-
-
-def attend_near(place, qn, own, other):
+
+
+STATE = jax.ShapeDtypeStruct((QHEADS * QROWS, HD), F32)
+WHOLE = pltpu.VMEM((SHARD, 2 * HD), BF16)
+
+
+def near_kernel(
+    place_ref, qn, qn_other, first, second, weight_ref,
+    acc, total, acc_other, total_other, weight, shard, sem,
+):
+    copy = pltpu.make_async_copy(weight_ref, weight, sem)
+    copy.start()
+    limit, x, c = place_ref[0], place_ref[3], place_ref[4]
+    join(first, second, shard)
+    for ref in (acc, total, acc_other, total_other):
+        ref[...] = jnp.zeros_like(ref)
+    seen_blocks(limit, x, c, False, (0,), (shard,), qn_other, acc_other, total_other)
+    seen_blocks(limit, x, c, True, (0,), (shard,), qn, acc, total)
+    copy.wait()
+
+
+def attend_near(place, qn, qn_other, first, second, weight):
     return pl.pallas_call(
         near_kernel,
-        in_specs=[SMEM()] + [VMEM()] * 3,
-        out_specs=[VMEM()] * 2,
-        out_shape=list(STATE),
+        in_specs=[SMEM()] + [VMEM()] * 4 + [HBM()],
+        out_specs=[VMEM()] * 5,
+        out_shape=[STATE] * 4 + [jax.ShapeDtypeStruct(weight.shape, BF16)],
+        scratch_shapes=[WHOLE, pltpu.SemaphoreType.DMA],
+        compiler_params=params(20),
+    )(place, qn, qn_other, first, second, weight)
+
+
+def middle_kernel(place_ref, qn, qn_other, *refs):
+    before, parts, after, shards = refs[:4], refs[4:8], refs[8:12], refs[12:]
+    limit, x, c = place_ref[0], place_ref[3], place_ref[4]
+    for ref, out_ref in zip(before, after):
+        out_ref[...] = ref[...]
+    join(parts[0], parts[1], shards[0])
+    join(parts[2], parts[3], shards[1])
+    seen_blocks(limit, x, c, False, (1, 3), shards, qn_other, after[2], after[3])
+    seen_blocks(limit, x, c, True, (1, 3), shards, qn, after[0], after[1])
+
+
+def attend_middle(place, qn, qn_other, state, parts):
+    return pl.pallas_call(
+        middle_kernel,
+        in_specs=[SMEM()] + [VMEM()] * 10,
+        out_specs=[VMEM()] * 4,
+        out_shape=[STATE] * 4,
+        scratch_shapes=[WHOLE] * 2,
         compiler_params=params(16),
-    )(place, qn, own, other)
-
-
-def far_kernel(place_ref, qn, acc_ref, total_ref, *refs):
-    first, third, parts, (acc, total, second) = refs[0], refs[1], refs[2:6], refs[6:]
+    )(place, qn, qn_other, *state, *parts)
+
+
+def far_kernel(own, place_ref, qn, acc_ref, total_ref, first, second, out_ref, acc, total, shard):
+    limit, x, c = place_ref[0], place_ref[3], place_ref[4]
     acc[...] = acc_ref[...]
     total[...] = total_ref[...]
-    join(place_ref, parts, second)
-    seen_blocks(place_ref, 0, (1, 3, 2), (first, third, second), qn, acc, total)
-
-
-def attend_far(place, qn, acc, total, shards):
-    return pl.pallas_call(
-        far_kernel,
-        in_specs=[SMEM()] + [VMEM()] * 9,
-        out_specs=[VMEM()] * 2,
-        out_shape=list(STATE),
-        scratch_shapes=[pltpu.VMEM((SHARD, 2 * HD), BF16)],
-        compiler_params=params(16),
-    )(place, qn, acc, total, *shards)
-
-
-def last_kernel(place_ref, qn, acc_ref, total_ref, *refs):
-    first, third, parts, refs = refs[0], refs[1], refs[2:6], refs[6:]
-    weight_ref, out_ref, acc, total, attn, weight, second, sem = refs
-    copy = pltpu.make_async_copy(weight_ref, weight, sem)
-    copy.start()
-    acc[...] = acc_ref[...]
-    total[...] = total_ref[...]
-    join(place_ref, parts, second)
-    seen_blocks(place_ref, 1, (1, 3, 2), (first, third, second), qn, acc, total)
-    for h in range(QHEADS):
-        at = pl.ds(h * QROWS, QROWS)
-        whole = jnp.sum(total[at, :], axis=1, keepdims=True)
-        attn[:, h * HD : (h + 1) * HD] = (acc[at, :] / whole).astype(BF16)
-    copy.wait()
-    for n in range(8):
-        columns = slice(n * 512, (n + 1) * 512)
-        product = jnp.dot(attn[...], weight[:, columns], preferred_element_type=F32)
-        out_ref[:, :, columns] = product.astype(BF16).reshape(GROUPS, ROWS, 512)
-
-
-def attend_last(place, qn, acc, total, shards, weight):
-    return pl.pallas_call(
-        last_kernel,
-        in_specs=[SMEM()] + [VMEM()] * 9 + [HBM()],
+    join(first, second, shard)
+    seen_blocks(limit, x, c, own, (2,), (shard,), qn, acc, total)
+    out_ref[:, :HD] = acc[...]
+    out_ref[:, HD:] = total[...]
+
+
+def attend_far(own, place, qn, acc, total, first, second):
+    return pl.pallas_call(
+        functools.partial(far_kernel, own),
+        in_specs=[SMEM()] + [VMEM()] * 5,
         out_specs=VMEM(),
-        out_shape=jax.ShapeDtypeStruct((GROUPS, ROWS, WIDTH), BF16),
+        out_shape=jax.ShapeDtypeStruct((QHEADS * QROWS, 2 * HD), F32),
         scratch_shapes=[
             pltpu.VMEM((QHEADS * QROWS, HD), F32),
             pltpu.VMEM((QHEADS * QROWS, HD), F32),
-            pltpu.VMEM((QROWS, QHEADS * HD), BF16),
-            pltpu.VMEM((QHEADS * HD, WIDTH), BF16),
-            pltpu.VMEM((SHARD, 2 * HD), BF16),
-            pltpu.SemaphoreType.DMA,
+            WHOLE,
         ],
-        compiler_params=params(20),
-    )(place, qn, acc, total, *shards, weight)
+        compiler_params=params(16),
+    )(place, qn, acc, total, first, second)
+
+
+def project_kernel(own_ref, other_ref, weight, out_ref, attn):
+    for h in range(QHEADS):
+        at = pl.ds(h * QROWS, QROWS)
+        both = own_ref[at, :] + other_ref[at, :]
+        whole = jnp.sum(both[:, HD:], axis=1, keepdims=True)
+        attn[:, h * HD : (h + 1) * HD] = (both[:, :HD] / whole).astype(BF16)
+    for n in range(8):
+        part = slice(n * 512, (n + 1) * 512)
+        product = jnp.dot(attn[...], weight[:, part], preferred_element_type=F32)
+        out_ref[:, :, part] = product.astype(BF16).reshape(GROUPS, ROWS, 512)
+
+
+def project(own, other, weight):
+    return pl.pallas_call(
+        project_kernel,
+        in_specs=[VMEM()] * 3,
+        out_specs=VMEM(),
+        out_shape=jax.ShapeDtypeStruct((GROUPS, ROWS, WIDTH), BF16),
+        scratch_shapes=[pltpu.VMEM((QROWS, QHEADS * HD), BF16)],
+        compiler_params=params(16),
+    )(own, other, weight)
 
 
 def route_kernel(
-    ids_hbm, weights_hbm, q_ref, gain_ref, placing_ref, mixing_ref, qn,
+    ids_hbm, weights_hbm, q_ref, gain_ref, other_ref, placing_ref, mixing_ref, qn, qn_other,
     ids_ref, weights_ref, queries, gain, sems,
 ):
     pairs = ((gain_ref, gain), (q_ref, queries), (ids_hbm, ids_ref), (weights_hbm, weights_ref))
@@ -275,18 +283,19 @@
             slot = jnp.where(before == s, held, 0.0).astype(BF16)
             table = table + jnp.dot(pick, slot, preferred_element_type=F32)
         out_ref[...] = jnp.where(same, table, 0.0).astype(BF16)
-    for h in range(QHEADS):
-        head = queries[:, h * HD : (h + 1) * HD].astype(F32)
-        qn[pl.ds(h * QROWS, QROWS), :] = rms_scale(head, gain[...]).astype(BF16)
-
-
-def route(expert_ids, combine_weight, queries, q_gain):
+    for ref, out_ref in ((queries, qn), (other_ref, qn_other)):
+        for h in range(QHEADS):
+            head = ref[:, h * HD : (h + 1) * HD].astype(F32)
+            out_ref[pl.ds(h * QROWS, QROWS), :] = rms_scale(head, gain[...]).astype(BF16)
+
+
+def route(expert_ids, combine_weight, queries, q_gain, other):
     return pl.pallas_call(
         route_kernel,
-        in_specs=[HBM()] * 4,
-        out_specs=[VMEM()] * 3,
+        in_specs=[HBM()] * 4 + [VMEM()],
+        out_specs=[VMEM()] * 4,
         out_shape=[jax.ShapeDtypeStruct((EXPERTS * LINES, EXPERTS), BF16)] * 2
-        + [jax.ShapeDtypeStruct((QHEADS * QROWS, HD), BF16)],
+        + [jax.ShapeDtypeStruct((QHEADS * QROWS, HD), BF16)] * 2,
         scratch_shapes=[
             pltpu.VMEM((8, ROWS), jnp.int32),
             pltpu.VMEM((8, ROWS), BF16),
@@ -295,7 +304,7 @@
             pltpu.SemaphoreType.DMA((4,)),
         ],
         compiler_params=params(16),
-    )(expert_ids, combine_weight, queries, q_gain)
+    )(expert_ids, combine_weight, queries, q_gain, other)
 
 
 def dispatch_kernel(parts_ref, residual_ref, gain_ref, placing_ref, hidden_ref, out_ref, pieces):
@@ -428,25 +437,26 @@
     z, y, x, c = (lax.axis_index(name).astype(jnp.int32) for name in ("z", "y", "x", "c"))
     place = jnp.stack([prefix_len[0], z, y, x, c])
     held = functools.partial(pltpu.with_memory_space_constraint, memory_space=pltpu.HBM)
-    own, part = prep(place, held(cache), held(new_kv), held(k_gain.reshape(1, HD)))
     swap = functools.partial(lax.ppermute, axis_name="c", perm=[(0, 1), (1, 0)])
-    other = swap(own)
-    parts = [lax.ppermute(part, "x", shift(2))]
-    placing, mixing, qn = route(
-        held(expert_ids.T), held(combine_weight.T), held(queries), held(q_gain.reshape(1, HD))
-    )
-    whole, parts[0], placing, mixing, qn = lax.optimization_barrier(
-        (own, parts[0], placing, mixing, qn)
-    )
-    part = swap(parts[0])
-    near = [lax.ppermute(whole, "x", shift(k)) for k in (1, 3)]
-    parts += [lax.ppermute(parts[0], "y", shift(k)) for k in (1, 2, 3)]
-    acc, total = attend_near(place, qn, own, other)
-    near = near + parts
-    *near, qn, acc, total = lax.optimization_barrier((*near, qn, acc, total))
-    far = [swap(near[0]), swap(near[1]), part] + [swap(shard) for shard in near[3:]]
-    acc, total = attend_far(place, qn, acc, total, near)
-    parts = attend_last(place, qn, acc, total, far, held(out_weight))
+    other = swap(queries)
+    left, right = shift(1), shift(3)
+    own = prep(place, held(cache), held(new_kv), held(k_gain.reshape(1, HD)))
+    first_left, second_right = lax.ppermute(own[0], "x", left), lax.ppermute(own[1], "x", right)
+    second_left, first_right = lax.ppermute(own[1], "x", left), lax.ppermute(own[0], "x", right)
+    placing, mixing, qn, qn_other = route(
+        held(expert_ids.T), held(combine_weight.T), held(queries), held(q_gain.reshape(1, HD)), other
+    )
+    first_left, second_right, placing, mixing, qn, qn_other = lax.optimization_barrier(
+        (first_left, second_right, placing, mixing, qn, qn_other)
+    )
+    first, second = lax.ppermute(first_left, "x", left), lax.ppermute(second_right, "x", right)
+    *state, weight = attend_near(place, qn, qn_other, *own, held(out_weight))
+    parts = (first_left, second_left, first_right, second_right)
+    acc, total, acc_other, total_other = attend_middle(place, qn, qn_other, state, parts)
+    far = attend_far(False, place, qn_other, acc_other, total_other, first, second)
+    far, acc, total = lax.optimization_barrier((far, acc, total))
+    mine = attend_far(True, place, qn, acc, total, first, second)
+    parts = project(mine, swap(far), weight)
     parts = lax.all_to_all(parts, ("z", "y"), split_axis=0, concat_axis=0, tiled=True)
     hidden, lines = dispatch(parts, residual, norm_gain.reshape(1, WIDTH), placing)
     everyone = ("z", "y", "x", "c")

time: 151 us -> 146 us (0.967)
  waiting for transfers between devices: 3.83 us -> 1 us
    ppermute x13 -> x8, waiting for transfers between devices: 3.83 us -> 1 us  [the longest x1 0.84 us: per_device(): parts = project(mine, swap(far), weight)]
    pallas_call x4 -> x6, Pallas kernels: 12.7 us -> 11.6 us  [the longest x2 2.87 us: attend_far(): pl.pallas_call(functools.partial(far_kernel, own), in_specs=[SMEM()] + [V...]
    ppermute x13 -> x8, starting transfers between devices: 14.4 us -> 13.7 us  [the longest x1 4.2 us: per_device(): parts = project(mine, swap(far), weight)]
  transfers between devices with their start and end apart: 13 -> 8, of which waited for: 4 -> 2; matrix products, arithmetic and copies ran while one was open for 0% -> 0% of each run, Pallas kernels for 6% -> 7%
where the time goes in v4:
time: 146 us; the launch traced here: 145 us
  blocking collectives  107 us (73%)
  Pallas kernels  22.4 us (15%)
  starting transfers between devices  13.7 us (9%)
    all_to_all x2, blocking collectives, per_device(): lax.all_to_all(lines, everyone, split_axis=0, concat_axis=0, tiled=True)  72 us
    all_to_all x1, blocking collectives, per_device(): lax.all_to_all(parts, ('z', 'y'), split_axis=0, concat_axis=0, tiled=True)  35.4 us
    pallas_call x1, Pallas kernels, experts(): pl.pallas_call(expert_kernel, in_specs=[VMEM(), VMEM(), HBM()], out_specs...  6.83 us
    ppermute x1, starting transfers between devices, per_device(): parts = project(mine, swap(far), weight)  4.2 us
  transfers between devices with their start and end apart: 8, of which 2 were waited for; matrix products, arithmetic and copies ran while one was open for 0% of the time, Pallas kernels for 7%

profile of v4, /device:TPU:1, one launch (start us, length us, event | category | flops | bytes accessed | tf_op | source)
XLA Modules:
  0.0 145.5 jit_solution(6639699198628171748)
XLA Ops:
  0.0 1.4 collective-permute-start.2
  2.1 0.1 stack.19.place_ref
  2.2 1.8 %shard_map.127 = (bf16[384,256]{1,0:T(8,128)(2,1)S(1)}, bf16[384,256]{1,0:T(8,128)(2,1)S(1)}) custom-call(s32[5]{0:T(128)S(1)} %stack.19.place_ref, bf16[4,512,256]{2,1,0:T(8,128)(2,1)} %cache_ref.1, bf16[4,256,256]{2,1,0:T(8,128)(2,1)} %new_ref.1, f32[1,128]{1,0:T(1,128)} %bitcast.20), custom_call_target="tpu_custom_call" | custom-call | tf_op jit(solution)/shard_map/pallas_call | solution.py:80
  3.9 1.4 collective-permute-start
  5.3 1.4 collective-permute-start.1
  6.7 0.1 collective-permute-start.3
  6.8 2.6 %collective-permute-start.4 = (bf16[384,256]{1,0:T(8,128)(2,1)S(1)}, bf16[384,256]{1,0:T(8,128)(2,1)S(1)}, u32[]{:S(2)}, u32[]{:S(2)}) collective-permute-start(bf16[384,256]{1,0:T(8,128)(2,1)S(1)} %get-tuple-element.31.first), channel_id=1, source_target_pairs={{0,6},{2,0},{4,2},{6,4},{1,7},{3,1},{5,3},{7,5},{8,14},{10,8},{12,... | collective-permute-start | bytes 589832 | tf_op jit(solution)/shard_map/ppermute | solution.py:445
  9.3 2.2 %shard_map.128 = (bf16[2048,128]{1,0:T(8,128)(2,1)S(1)}, bf16[2048,128]{1,0:T(8,128)(2,1)S(1)}, bf16[1024,128]{1,0:T(8,128)(2,1)S(1)}, bf16[1024,128]{1,0:T(8,128)(2,1)S(1)}) custom-call(s32[8,16]{1,0:T(8,128)} %bitcast.18, bf16[8,16]{1,0:T(8,128)(2,1)} %bitcast.19, bf16[256,512]{1,0:T(8,128)(2,1)} %q_ref.1, f32[1,128]{1,0:T(1,128)} %bitcast.21, ...), custom_call_target="tpu_custom_call" | custom-call | tf_op jit(solution)/shard_map/pallas_call | solution.py:293
  11.6 0.1 collective-permute-done.refs_4_
  11.7 1.0 collective-permute-start.5
  12.7 1.7 %collective-permute-start.6 = (bf16[384,256]{1,0:T(8,128)(2,1)S(1)}, bf16[384,256]{1,0:T(8,128)(2,1)S(1)}, u32[]{:S(2)}, u32[]{:S(2)}) collective-permute-start(bf16[384,256]{1,0:T(8,128)(2,1)S(1)} %collective-permute-done.1.refs_7_), channel_id=1, source_target_pairs={{0,6},{2,0},{4,2},{6,4},{1,7},{3,1},{5,3},{7,5},{8,14},{10,8},{12,... | collective-permute-start | bytes 589832 | tf_op jit(solution)/shard_map/ppermute | solution.py:452
  14.4 2.7 %shard_map.129 = (f32[1024,128]{1,0:T(8,128)S(1)}, f32[1024,128]{1,0:T(8,128)S(1)}, f32[1024,128]{1,0:T(8,128)S(1)}, f32[1024,128]{1,0:T(8,128)S(1)}, bf16[512,4096]{1,0:T(8,128)(2,1)S(1)}) custom-call(s32[5]{0:T(128)S(1)} %stack.19.place_ref, bf16[1024,128]{1,0:T(8,128)(2,1)S(1)} %get-tuple-element.37.qn, ...), custom_call_target="tpu_custom_call" | custom-call | tf_op jit(solution)/shard_map/pallas_call | solution.py:165
  17.2 2.4 %shard_map.130 = (f32[1024,128]{1,0:T(8,128)S(1)}, f32[1024,128]{1,0:T(8,128)S(1)}, f32[1024,128]{1,0:T(8,128)S(1)}, f32[1024,128]{1,0:T(8,128)S(1)}) custom-call(s32[5]{0:T(128)S(1)} %stack.19.place_ref, bf16[1024,128]{1,0:T(8,128)(2,1)S(1)} %get-tuple-element.37.qn, bf16[1024,128]{1,0:T(8,128)(2,1)S(1)} %get-tuple-element.38.qn_other.qn, ...), custom_call_target="tpu_custom_call" | custom-call | tf_op jit(solution)/shard_map/pallas_call | solution.py:187
  19.7 1.4 shard_map.131
  21.1 4.2 %collective-permute-start.7 = (f32[1024,256]{1,0:T(8,128)S(1)}, f32[1024,256]{1,0:T(8,128)S(1)}, u32[]{:S(2)}, u32[]{:S(2)}) collective-permute-start(f32[1024,256]{1,0:T(8,128)S(1)} %shard_map.131), channel_id=1, source_target_pairs={{0,1},{1,0},{2,3},{3,2},{4,5},{5,4},{6,7},{7,6},{8,9},{9,8},{10,11... | collective-permute-start | bytes 3145736 | tf_op jit(solution)/shard_map/ppermute | solution.py:459
  25.3 1.4 shard_map.132.own_ref
  26.7 0.8 collective-permute-done.7.other_ref
  27.6 1.4 shard_map.133
  29.0 35.4 %all_to_all.15.parts_ref = bf16[16,16,4096]{2,1,0:T(8,128)(2,1)S(1)} all-to-all(bf16[16,16,4096]{2,1,0:T(8,128)(2,1)S(1)} %shard_map.133), channel_id=1, replica_groups=mesh['z'=4,'y'=4,'x'=4,'c'=2] {'z','y'}, dimensions={0} | all-to-all | bytes 4194304 | tf_op jit(solution)/shard_map/all_to_all | solution.py:460
  64.4 1.1 shard_map.134
  65.5 37.6 %all_to_all.16.lines_ref = bf16[128,16,512]{2,1,0:T(8,128)(2,1)S(1)} all-to-all(bf16[128,16,512]{2,1,0:T(8,128)(2,1)S(1)} %get-tuple-element.54), channel_id=1, replica_groups=mesh['z'=4,'y'=4,'x'=4,'c'=2] {'z','y','x','c'}, dimensions={0} | all-to-all | bytes 4194304 | tf_op jit(solution)/shard_map/all_to_all | solution.py:463
  103.1 6.8 %shard_map.135 = bf16[128,16,512]{2,1,0:T(8,128)(2,1)S(1)} custom-call(bf16[128,16,512]{2,1,0:T(8,128)(2,1)S(1)} %all_to_all.16.lines_ref, bf16[4096,1536]{1,0:T(8,128)(2,1)S(1)} %bitcast.13, bf16[768,4096]{1,0:T(8,128)(2,1)S(1)} %bitcast.16), custom_call_target="tpu_custom_call" | custom-call | tf_op jit(solution)/shard_map/pallas_call | solution.py:384
  109.9 34.4 %all_to_all.17.lines_ref = bf16[128,16,512]{2,1,0:T(8,128)(2,1)S(1)} all-to-all(bf16[128,16,512]{2,1,0:T(8,128)(2,1)S(1)} %shard_map.135), channel_id=1, replica_groups=mesh['z'=4,'y'=4,'x'=4,'c'=2] {'z','y','x','c'}, dimensions={0} | all-to-all | bytes 4194304 | tf_op jit(solution)/shard_map/all_to_all | solution.py:465
  144.3 1.1 shard_map.136
  (22 shorter events, 0.1 us)
Async XLA Ops:
  0.0 9.3 %collective-permute-start.2 = (bf16[256,512]{1,0:T(8,128)(2,1)}, bf16[256,512]{1,0:T(8,128)(2,1)S(1)}, u32[]{:S(2)}, u32[]{:S(2)}) collective-permute-start(bf16[256,512]{1,0:T(8,128)(2,1)} %q_ref.1), channel_id=1, source_target_pairs={{0,1},{1,0},{2,3},{3,2},{4,5},{5,4},{6,7},{7,6},{8,9},{9,8},{10,11... | collective-permute-start | bytes 786440 | tf_op jit(solution)/shard_map/ppermute | solution.py:441
  3.9 7.8 %collective-permute-start = (bf16[384,256]{1,0:T(8,128)(2,1)S(1)}, bf16[384,256]{1,0:T(8,128)(2,1)S(1)}, u32[]{:S(2)}, u32[]{:S(2)}) collective-permute-start(bf16[384,256]{1,0:T(8,128)(2,1)S(1)} %get-tuple-element.31.first), channel_id=1, source_target_pairs={{0,2},{2,4},{4,6},{6,0},{1,3},{3,5},{5,7},{7,1},{8,10},{10,12},{12... | collective-permute-start | bytes 589832 | tf_op jit(solution)/shard_map/ppermute | solution.py:444
  5.3 6.5 %collective-permute-start.1 = (bf16[384,256]{1,0:T(8,128)(2,1)S(1)}, bf16[384,256]{1,0:T(8,128)(2,1)S(1)}, u32[]{:S(2)}, u32[]{:S(2)}) collective-permute-start(bf16[384,256]{1,0:T(8,128)(2,1)S(1)} %get-tuple-element.32.second), channel_id=1, source_target_pairs={{0,6},{2,0},{4,2},{6,4},{1,7},{3,1},{5,3},{7,5},{8,14},{10,8},{12,... | collective-permute-start | bytes 589832 | tf_op jit(solution)/shard_map/ppermute | solution.py:444
  6.7 10.5 %collective-permute-start.3 = (bf16[384,256]{1,0:T(8,128)(2,1)S(1)}, bf16[384,256]{1,0:T(8,128)(2,1)S(1)}, u32[]{:S(2)}, u32[]{:S(2)}) collective-permute-start(bf16[384,256]{1,0:T(8,128)(2,1)S(1)} %get-tuple-element.32.second), channel_id=1, source_target_pairs={{0,2},{2,4},{4,6},{6,0},{1,3},{3,5},{5,7},{7,1},{8,10},{10,12},{12... | collective-permute-start | bytes 589832 | tf_op jit(solution)/shard_map/ppermute | solution.py:445
  6.8 10.4 %collective-permute-start.4 = (bf16[384,256]{1,0:T(8,128)(2,1)S(1)}, bf16[384,256]{1,0:T(8,128)(2,1)S(1)}, u32[]{:S(2)}, u32[]{:S(2)}) collective-permute-start(bf16[384,256]{1,0:T(8,128)(2,1)S(1)} %get-tuple-element.31.first), channel_id=1, source_target_pairs={{0,6},{2,0},{4,2},{6,4},{1,7},{3,1},{5,3},{7,5},{8,14},{10,8},{12,... | collective-permute-start | bytes 589832 | tf_op jit(solution)/shard_map/ppermute | solution.py:445
  11.7 7.9 %collective-permute-start.5 = (bf16[384,256]{1,0:T(8,128)(2,1)S(1)}, bf16[384,256]{1,0:T(8,128)(2,1)S(1)}, u32[]{:S(2)}, u32[]{:S(2)}) collective-permute-start(bf16[384,256]{1,0:T(8,128)(2,1)S(1)} %collective-permute-done.refs_4_), channel_id=1, source_target_pairs={{0,2},{2,4},{4,6},{6,0},{1,3},{3,5},{5,7},{7,1},{8,10},{10,12},{12... | collective-permute-start | bytes 589832 | tf_op jit(solution)/shard_map/ppermute | solution.py:452
  12.7 6.9 %collective-permute-start.6 = (bf16[384,256]{1,0:T(8,128)(2,1)S(1)}, bf16[384,256]{1,0:T(8,128)(2,1)S(1)}, u32[]{:S(2)}, u32[]{:S(2)}) collective-permute-start(bf16[384,256]{1,0:T(8,128)(2,1)S(1)} %collective-permute-done.1.refs_7_), channel_id=1, source_target_pairs={{0,6},{2,0},{4,2},{6,4},{1,7},{3,1},{5,3},{7,5},{8,14},{10,8},{12,... | collective-permute-start | bytes 589832 | tf_op jit(solution)/shard_map/ppermute | solution.py:452
  19.6 83.4 %slice-start = ((s8[12582912]{0:T(1024)(128)(4,1)}), s8[4194304]{0:T(1024)(128)(4,1)S(1)}, s32[]{:S(2)}) async-start(s8[12582912]{0:T(1024)(128)(4,1)} %bitcast.11), calls=%async_computation.3 | async-start | bytes 8388608
  19.6 83.4 %slice-start.3 = ((s8[6291456]{0:T(1024)(128)(4,1)}), s8[4194304]{0:T(1024)(128)(4,1)S(1)}, s32[]{:S(2)}) async-start(s8[6291456]{0:T(1024)(128)(4,1)} %bitcast.14), calls=%async_computation.6 | async-start | bytes 8388608
  21.1 6.5 %collective-permute-start.7 = (f32[1024,256]{1,0:T(8,128)S(1)}, f32[1024,256]{1,0:T(8,128)S(1)}, u32[]{:S(2)}, u32[]{:S(2)}) collective-permute-start(f32[1024,256]{1,0:T(8,128)S(1)} %shard_map.131), channel_id=1, source_target_pairs={{0,1},{1,0},{2,3},{3,2},{4,5},{5,4},{6,7},{7,6},{8,9},{9,8},{10,11... | collective-permute-start | bytes 3145736 | tf_op jit(solution)/shard_map/ppermute | solution.py:459
  27.6 36.8 %copy-start = (bf16[16,4096]{1,0:T(8,128)(2,1)S(1)}, bf16[16,4096]{1,0:T(8,128)(2,1)}, u32[]{:S(2)}) copy-start(bf16[16,4096]{1,0:T(8,128)(2,1)} %residual_ref.1) | copy-start | bytes 393220
  27.6 36.8 %copy-start.1 = (f32[4096]{0:T(1024)S(1)}, f32[4096]{0:T(1024)}, u32[]{:S(2)}) copy-start(f32[4096]{0:T(1024)} %param.20) | copy-start | bytes 49156
  27.6 75.5 %slice-start.1 = ((s8[12582912]{0:T(1024)(128)(4,1)}), s8[4194304]{0:T(1024)(128)(4,1)S(1)}, s32[]{:S(2)}) async-start(s8[12582912]{0:T(1024)(128)(4,1)} %bitcast.11), calls=%async_computation.4 | async-start | bytes 8388608
  27.6 75.5 %slice-start.4 = ((s8[6291456]{0:T(1024)(128)(4,1)}), s8[2097152]{0:T(1024)(128)(4,1)S(1)}, s32[]{:S(2)}) async-start(s8[6291456]{0:T(1024)(128)(4,1)} %bitcast.14), calls=%async_computation.7 | async-start | bytes 4194304
  29.0 74.1 %slice-start.2 = ((s8[12582912]{0:T(1024)(128)(4,1)}), s8[4194304]{0:T(1024)(128)(4,1)S(1)}, s32[]{:S(2)}) async-start(s8[12582912]{0:T(1024)(128)(4,1)} %bitcast.11), calls=%async_computation.5 | async-start | bytes 8388608
